TPU v7x, 32 devices: a whole 2x2x4 slice. The times are simulated.
32 devices in a mesh: groups: 2 (over y), space: 16 (over z, x, core).
Axes of the slice: x: 2, y: 2, z: 4, core: 2. Of those that a mesh axis runs over, the one named last changes fastest.
Arguments:
- field: bfloat16 [2, 16, 256, 256, 128], P('groups', None, 'space'), parts along dimension 0, may hold values from -6 to 6
- cotangent: bfloat16 [2, 16, 256, 256, 128], P('groups', None, 'space'), parts along dimension 0, may hold values from -6 to 6
- spectral_weight: bfloat16 [2, 16, 16, 64, 2048], P(None, None, None, None, 'space'), may hold values from -3 to 3
- point_weight: bfloat16 [16, 16], replicated, may hold values from -1.5 to 1.5
- bias: float32 [16], replicated, may hold values from -1 to 1
Outputs:
- activation: bfloat16 [2, 16, 256, 256, 128], P('groups', None, 'space'), parts along dimension 0
- grad_field: bfloat16 [2, 16, 256, 256, 128], P('groups', None, 'space'), parts along dimension 0
- grad_spectral: float32 [4, 16, 16, 64, 2048], P('groups', None, None, None, 'space'), parts along dimension 0
- grad_point: float32 [32, 16], P('groups'), parts along dimension 0
- grad_bias: float32 [32], P('groups'), parts along dimension 0
There are 2 independent parts, one for each index of `groups`. A program takes and returns all parts, laid end to end along the dimension named above; an argument that names none is the same for every part. Nothing has to cross between parts.
All inputs are finite; a program needn't handle non-finite values.
Results may differ from a plain program's by a relative error of at most 0.0094.
Values sent between devices are 32-bit elements; how exact they have to be, the bound alone decides.
A program may use at most 320 MiB of HBM per device.

v0:
```python
import math

import jax
import jax.numpy as jnp
from jax import lax
from jax.sharding import PartitionSpec as P

MODES = 32


TURN = 2.0 * math.pi
GELU_SCALE = math.sqrt(2.0 / math.pi)
GELU_CUBE = 0.044715
PRECISE = lax.Precision.HIGHEST


def twiddle(length, frequencies):
    places = jnp.arange(length, dtype=jnp.int32)[:, None]
    phase = (places * frequencies[None, :] % length).astype(jnp.float32) * (TURN / length)
    factor = 1.0 / math.sqrt(length)
    return (jnp.cos(phase) * factor, -jnp.sin(phase) * factor)


def kept_modes(length, modes):
    return jnp.concatenate(
        [jnp.arange(modes, dtype=jnp.int32), jnp.arange(length - modes, length, dtype=jnp.int32)]
    )


def block_table(real_part, imag_part):
    upper = jnp.stack([real_part, imag_part], axis=1)
    lower = jnp.stack([-imag_part, real_part], axis=1)
    return jnp.stack([upper, lower], axis=1)


def make_tables(cells_x, cells_y, cells_z, modes):
    z_real, z_imag = twiddle(cells_z, jnp.arange(modes, dtype=jnp.int32))
    forward_z = jnp.concatenate([z_real, z_imag], axis=1)
    doubling = jnp.where(jnp.arange(modes, dtype=jnp.int32) == 0, 1.0, 2.0).astype(jnp.float32)
    double_z = forward_z * jnp.concatenate([doubling, doubling])[None, :]
    y_real, y_imag = twiddle(cells_y, kept_modes(cells_y, modes))
    full_y = block_table(y_real, y_imag)
    x_real, x_imag = twiddle(cells_x, kept_modes(cells_x, modes))
    full_x = block_table(x_real, x_imag)
    return (
        forward_z.astype(jnp.bfloat16),
        double_z.astype(jnp.bfloat16),
        full_y.astype(jnp.bfloat16),
        full_y,
        full_x,
    )


def analyse_slab(values, z_table, y_table):
    zspec = jnp.dot(values, z_table, preferred_element_type=jnp.float32).astype(jnp.bfloat16)
    shape = zspec.shape
    split_values = zspec.reshape(shape[:4] + (2, shape[4] // 2))
    result = jnp.einsum(
        "bcxyrk,yrsq->bcxsqk", split_values, y_table, preferred_element_type=jnp.float32
    )
    rshape = result.shape
    return result.reshape(rshape[:4] + (rshape[4] * rshape[5],))


def restore_slab(values, y_table, z_table):
    shape = values.shape
    modes_y = y_table.shape[3]
    split_values = values.reshape(shape[:4] + (modes_y, shape[4] // modes_y))
    result = jnp.einsum("bcxrqk,ysrq->bcxysk", split_values, y_table, precision=PRECISE)
    rshape = result.shape
    rounded = result.reshape(rshape[:4] + (rshape[4] * rshape[5],)).astype(jnp.bfloat16)
    return jnp.dot(rounded, z_table.T, preferred_element_type=jnp.float32)


def x_forward(values, table):
    return jnp.einsum("bcxrm,xrsq->bcsqm", values, table, precision=PRECISE)


def x_inverse(values, table):
    return jnp.einsum("bcrqm,xsrq->bcxsm", values, table, precision=PRECISE)


def gelu_parts(preact):
    cube = preact * preact * preact
    tangent = jnp.tanh(GELU_SCALE * (preact + GELU_CUBE * cube))
    value = 0.5 * preact * (1.0 + tangent)
    slope = 0.5 * (1.0 + tangent) + 0.5 * preact * (1.0 - tangent * tangent) * GELU_SCALE * (
        1.0 + 3.0 * GELU_CUBE * preact * preact
    )
    return (value, slope)


def contract(form, left, right):
    return jnp.einsum(form, left, right, preferred_element_type=jnp.float32)


def mix_forward(spectrum, weight):
    u_real, u_imag = (spectrum[:, :, 0], spectrum[:, :, 1])
    w_real, w_imag = (weight[0], weight[1])
    form = "bikm,iokm->bokm"
    out_real = contract(form, u_real, w_real) - contract(form, u_imag, w_imag)
    out_imag = contract(form, u_real, w_imag) + contract(form, u_imag, w_real)
    return jnp.stack([out_real, out_imag], axis=2)


def mix_dual(grads, weight):
    g_real, g_imag = (grads[:, :, 0], grads[:, :, 1])
    w_real, w_imag = (weight[0], weight[1])
    form = "bokm,iokm->bikm"
    in_real = contract(form, g_real, w_real) + contract(form, g_imag, w_imag)
    in_imag = contract(form, g_imag, w_real) - contract(form, g_real, w_imag)
    return jnp.stack([in_real, in_imag], axis=2)


def weight_grad(spectrum, grads):
    u_real, u_imag = (spectrum[:, :, 0], spectrum[:, :, 1])
    g_real, g_imag = (grads[:, :, 0], grads[:, :, 1])
    form = "bikm,bokm->iokm"
    part_real = contract(form, u_real, g_real) + contract(form, u_imag, g_imag)
    part_imag = contract(form, u_real, g_imag) - contract(form, u_imag, g_real)
    return jnp.stack([part_real, part_imag], axis=0)


def body(field, cotangent, spectral_weight, point_weight, bias):
    spaces = lax.axis_size("space")
    planes = field.shape[2]
    cells_y = field.shape[3]
    cells_z = field.shape[4]
    cells_x = planes * spaces
    forward_z, double_z, half_y, full_y, full_x = make_tables(cells_x, cells_y, cells_z, MODES)

    def x_step(values):
        return x_forward(values, full_x)

    spectrum = analyse_slab(field, forward_z, half_y)
    owned = x_step(lax.all_to_all(spectrum, "space", split_axis=4, concat_axis=2, tiled=True))
    owned_low = owned.astype(jnp.bfloat16)
    mixed = mix_forward(owned_low, spectral_weight)
    xback = x_inverse(mixed, full_x)
    returned = lax.all_to_all(xback, "space", split_axis=2, concat_axis=4, tiled=True)
    spectral_part = restore_slab(returned, full_y, double_z)
    pointwise = contract("oi,bixyz->boxyz", point_weight.T, field)
    preact = spectral_part + pointwise + bias[None, :, None, None, None]
    value, slope = gelu_parts(preact)
    activation = value.astype(jnp.bfloat16)
    grad_low = (cotangent.astype(jnp.float32) * slope).astype(jnp.bfloat16)
    point_sum = contract("bixyz,boxyz->io", field, grad_low)
    bias_sum = jnp.sum(grad_low, axis=(0, 2, 3, 4), dtype=jnp.float32)
    point_total, bias_total = lax.psum((point_sum, bias_sum), "space")
    grad_spec = analyse_slab(grad_low, double_z, half_y)
    grad_owned = x_step(lax.all_to_all(grad_spec, "space", split_axis=4, concat_axis=2, tiled=True))
    grad_owned_low = grad_owned.astype(jnp.bfloat16)
    grad_spectral = weight_grad(owned_low, grad_owned_low)
    dual = mix_dual(grad_owned_low, spectral_weight)
    dxback = x_inverse(dual, full_x)
    dreturned = lax.all_to_all(dxback, "space", split_axis=2, concat_axis=4, tiled=True)
    spectral_grad = restore_slab(dreturned, full_y, forward_z)
    total = spectral_grad + contract("io,boxyz->bixyz", point_weight, grad_low)
    grad_field = total.astype(jnp.bfloat16)
    factor = 1.0 / math.sqrt(cells_x * cells_y * cells_z)
    return (activation, grad_field, grad_spectral, point_total * factor, bias_total * factor)


def solution(mesh):
    placed = (
        P("groups", None, "space", None, None),
        P("groups", None, "space", None, None),
        P(None, None, None, None, "space"),
        P(),
        P(),
    )
    return jax.shard_map(
        body,
        mesh=mesh,
        in_specs=placed,
        out_specs=(
            P("groups", None, "space", None, None),
            P("groups", None, "space", None, None),
            P("groups", None, None, None, "space"),
            P("groups", None),
            P("groups"),
        ),
        check_vma=False,
    )
```

profile of v0, /device:TPU:16, one launch (start us, length us, event | category | flops | bytes accessed | tf_op | source)
XLA Modules:
  0.0 1153.2 jit_solution(7199986691230224915)
XLA Ops:
  1.2 11.5 convolution_convert_fusion
  12.7 10.1 convolution_bitcast_fusion.1
  22.7 45.0 %copy.158 = f32[1,16,16,2,64,32]{2,3,1,5,4,0:T(2,128)} copy(f32[1,16,16,2,64,32]{4,5,2,1,3,0:T(8,128)} %convolution_bitcast_fusion.1) | data formatting | bytes 8388608 | tf_op jit(solution)/shard_map/reshape | solution.py:62
  67.7 47.2 %reshape.335 = f32[16,1,65536]{2,1,0:T(1,128)} reshape(f32[2048,1,16,2,16]{4,3,2,1,0:T(2,128)} %bitcast.301) | data formatting | bytes 8388608
  114.9 6.5 all-to-all-start
  121.5 92.5 %all-to-all-done = f32[16,1,65536]{2,1,0:T(1,128)} async-done(((f32[16,1,65536]{2,1,0:T(1,128)}), f32[16,1,65536]{2,1,0:T(1,128)}, u32[]{:S(2)}, u32[]{:S(2)}) %all-to-all-start) | async-done | bytes 4194336 | tf_op jit(solution)/shard_map/all_to_all | solution.py:136
  214.4 14.0 %reduce.16 = f32[16,65536]{1,0:T(8,128)} reduce(f32[16,1,65536]{2,1,0:T(1,128)} %all-to-all-done, f32[]{:T(128)} %broadcast.252), dimensions={1}, to_apply=%all_to_all.44.reduce_sub_computation | reduce | bytes 8388612 | tf_op jit(solution)/shard_map/all_to_all | solution.py:136
  228.4 63.1 %reshape.336 = f32[2048,1,16,2,16]{4,3,2,1,0:T(2,128)} reshape(f32[16,65536]{1,0:T(8,128)} %reduce.16) | data formatting | bytes 8388608
  291.5 42.2 %copy.51 = f32[1,16,16,2,2048]{4,0,3,2,1:T(1,128)} copy(f32[1,16,16,2,2048]{2,3,1,0,4:T(2,128)} %bitcast.303) | data formatting | bytes 8388608 | tf_op jit(solution)/shard_map/all_to_all | solution.py:136
  333.8 5.6 copy.52
  339.4 2.3 fusion.39
  341.8 1.2 convert_bitcast_fusion.2
  343.0 3.7 fusion.24
  346.8 3.5 convolution_bitcast_fusion.3
  350.4 4.4 copy.54
  354.8 5.0 all-to-all-start.1
  359.9 22.3 %fusion.20 = f32[16,256,128,16]{2,3,1,0:T(8,128)} fusion(bf16[16,16,256,128]{3,2,1,0:T(8,128)(2,1)} %bitcast.307, bf16[16,16]{1,0:T(8,128)(2,1)S(1)} %copy-done), kind=kOutput, calls=%fused_computation.29 | convolution fusion | flops 268435456 | bytes 50332160 | tf_op jit(solution)/shard_map/oi,bixyz->boxyz/dot_general | solution.py:94
  382.3 70.1 %all-to-all-done.1 = f32[1,16,256,2,128]{4,1,3,0,2:T(8,128)} async-done(((f32[1,16,256,2,128]{4,1,3,0,2:T(8,128)}), f32[1,16,256,2,128]{4,1,3,0,2:T(8,128)}, u32[]{:S(2)}, u32[]{:S(2)}) %all-to-all-start.1) | async-done | bytes 4194336 | tf_op jit(solution)/shard_map/all_to_all | solution.py:140
  452.4 6.6 copy.198
  459.0 10.9 reshape.283
  469.9 40.5 %fusion.30 = bf16[1,16,16,256,2,32]{3,5,2,1,4,0:T(8,128)(2,1)} fusion(f32[16,16,2,64,32]{4,3,2,1,0:T(8,128)} %reshape.283, f32[256,2,2,64,1,1]{0,3,1,2,5,4:T(8,128)S(1)} %get-tuple-element.47), kind=kOutput, calls=%fused_computation.47 | convolution fusion | flops 6446645248 | bytes 12845056 | tf_op jit(solution)/shard_map/bcxrqk,ysrq->bcxysk/dot_general | solution.py:69
  510.4 8.1 copy.58
  518.4 50.8 %convert_reduce_fusion = (f32[16]{0:T(128)S(1)}, bf16[1,16,16,256,128]{4,3,2,1,0:T(8,128)(2,1)}, bf16[1,16,16,256,128]{4,3,2,1,0:T(8,128)(2,1)}) fusion(bf16[1,16,16,256,128]{4,3,2,1,0:T(8,128)(2,1)} %param.6, f32[16]{0:T(128)S(1)} %copy-done.7, f32[16,256,128,16]{2,3,1,0:T(8,128)} %fusion.20, bf16[16,16,256,64]{2,3,1,0:T(8,128)(2,1)} %bitcast.322, ...), kind=kOutput, calls=%fused_computation.15 | convolution fusion | flops 1291870208 | bytes 92307840 | tf_op jit(solution)/shard_map/dot_general | solution.py:72
  569.2 11.8 %convolution_convert_fusion.1 = bf16[16,16,256,64]{2,3,1,0:T(8,128)(2,1)S(1)} fusion(f32[128,32]{0,1:T(8,128)S(1)} %get-tuple-element.54, f32[128,32]{0,1:T(8,128)S(1)} %get-tuple-element.55, f32[64]{0:T(128)S(1)} %pad_maximum_fusion.5, bf16[1,16,16,256,128]{4,3,2,1,0:T(8,128)(2,1)} %get-tuple-element.35), kind=kOutput, calls=%fused_computation.52 | convolution fusion | flops 1077960704 | bytes 25198848 | tf_op jit(solution)/shard_map/dot_general | solution.py:55
  581.0 4.7 convolution_bitcast_fusion
  585.6 45.0 %copy.165 = f32[1,16,16,2,64,32]{2,3,1,5,4,0:T(2,128)} copy(f32[1,16,16,2,64,32]{4,5,2,1,3,0:T(8,128)} %convolution_bitcast_fusion) | data formatting | bytes 8388608 | tf_op jit(solution)/shard_map/reshape | solution.py:62
  630.6 47.2 %reshape.337 = f32[16,1,65536]{2,1,0:T(1,128)} reshape(f32[2048,1,16,2,16]{4,3,2,1,0:T(2,128)} %bitcast.302) | data formatting | bytes 8388608
  677.8 97.6 %all_to_all.60 = f32[16,1,65536]{2,1,0:T(1,128)} all-to-all(f32[16,1,65536]{2,1,0:T(1,128)} %reshape.337), channel_id=1, replica_groups=mesh['groups'=2,'space'=16] {'space'}, dimensions={0} | all-to-all | bytes 8388608 | tf_op jit(solution)/shard_map/all_to_all | solution.py:151
  775.4 14.0 %reduce.17 = f32[16,65536]{1,0:T(8,128)} reduce(f32[16,1,65536]{2,1,0:T(1,128)} %all_to_all.60, f32[]{:T(128)} %broadcast.252), dimensions={1}, to_apply=%all_to_all.50.reduce_sub_computation | reduce | bytes 8388612 | tf_op jit(solution)/shard_map/all_to_all | solution.py:151
  789.4 63.3 %reshape.338 = f32[2048,1,16,2,16]{4,3,2,1,0:T(2,128)} reshape(f32[16,65536]{1,0:T(8,128)} %reduce.17) | data formatting | bytes 8388608
  852.7 42.2 %copy.64 = f32[1,16,16,2,2048]{4,0,3,2,1:T(1,128)} copy(f32[1,16,16,2,2048]{2,3,1,0,4:T(2,128)} %bitcast.304) | data formatting | bytes 8388608 | tf_op jit(solution)/shard_map/all_to_all | solution.py:151
  894.9 5.6 copy.65
  900.5 2.3 fusion.38
  903.2 3.7 fusion.28
  907.0 3.5 convolution_bitcast_fusion.2
  910.5 4.4 copy.67
  915.0 5.0 all-to-all-start.3
  919.9 34.1 %fusion.40 = f32[16,16]{0,1:T(8,128)S(1)} fusion(bf16[16,16,256,128]{3,2,1,0:T(8,128)(2,1)} %bitcast.308, bf16[16,16,256,128]{3,2,1,0:T(8,128)(2,1)} %bitcast.305), kind=kOutput, calls=%fused_computation.65 | convolution fusion | flops 268435456 | bytes 33555456 | tf_op jit(solution)/shard_map/bixyz,boxyz->io/dot_general | solution.py:94
  954.0 77.6 %all-reduce = (f32[16,16]{0,1:T(8,128)S(1)}, f32[16]{0:T(128)S(1)}) all-reduce(f32[16,16]{0,1:T(8,128)S(1)} %fusion.40, f32[16]{0:T(128)S(1)} %get-tuple-element.34), channel_id=1, replica_groups=mesh['groups'=2,'space'=16] {'space'}, use_global_device_ids=true, to_apply=%region_0.1 | all-reduce | flops 272 | bytes 2176 | tf_op jit(solution)/shard_map/psum | solution.py:149
  1031.6 0.7 copy.76
  1032.8 22.4 %fusion.17 = f32[16,256,128,16]{2,3,1,0:T(8,128)} fusion(bf16[16,16,256,128]{3,2,1,0:T(8,128)(2,1)} %bitcast.306, bf16[16,16]{1,0:T(8,128)(2,1)S(1)} %copy-done), kind=kOutput, calls=%fused_computation.26 | convolution fusion | flops 268435456 | bytes 50332160 | tf_op jit(solution)/shard_map/io,boxyz->bixyz/dot_general | solution.py:94
  1055.2 2.4 add_bitcast_fusion
  1057.6 6.2 pad_maximum_fusion
  1063.8 6.6 copy.197
  1070.4 10.9 reshape.291
  1081.3 40.3 %fusion.31 = bf16[1,16,16,256,2,32]{3,5,2,1,4,0:T(8,128)(2,1)} fusion(f32[16,16,2,64,32]{4,3,2,1,0:T(8,128)} %reshape.291, f32[256,2,2,64,1,1]{0,3,1,2,5,4:T(8,128)S(1)} %copy-done.4), kind=kOutput, calls=%fused_computation.48 | convolution fusion | flops 6446645248 | bytes 12845056 | tf_op jit(solution)/shard_map/bcxrqk,ysrq->bcxysk/dot_general | solution.py:69
  1121.6 8.1 copy.71
  1129.6 23.4 %fusion.9 = bf16[1,16,16,256,128]{4,3,2,1,0:T(8,128)(2,1)} fusion(f32[16,256,128,16]{2,3,1,0:T(8,128)} %fusion.17, bf16[16,16,256,64]{2,3,1,0:T(8,128)(2,1)} %bitcast.310, f32[128,32]{0,1:T(8,128)S(1)} %get-tuple-element.54, f32[128,32]{0,1:T(8,128)S(1)} %get-tuple-element.55), kind=kOutput, calls=%fused_computation.12 | convolution fusion | flops 1090551808 | bytes 58753024 | tf_op jit(solution)/shard_map/dot_general | solution.py:72
  (44 shorter events, 2.2 us)
Async XLA Ops:
  0.6 359.3 %copy-start = (bf16[16,16]{1,0:T(8,128)(2,1)S(1)}, bf16[16,16]{1,0:T(8,128)(2,1)}, u32[]{:S(2)}) copy-start(bf16[16,16]{1,0:T(8,128)(2,1)} %param.8) | copy-start | bytes 1540
  114.9 99.0 %all-to-all-start = ((f32[16,1,65536]{2,1,0:T(1,128)}), f32[16,1,65536]{2,1,0:T(1,128)}, u32[]{:S(2)}, u32[]{:S(2)}) async-start(f32[16,1,65536]{2,1,0:T(1,128)} %reshape.335), calls=%async_computation | async-start | bytes 8388608 | tf_op jit(solution)/shard_map/all_to_all | solution.py:136
  121.4 225.4 %copy-start.1 = (f32[256,2,2,64,1]{0,3,1,2,4:T(8,128)}, f32[256,2,2,64,1]{0,3,1,2,4:T(8,128)S(1)}, u32[]{:S(2)}) copy-start(f32[256,2,2,64,1]{0,3,1,2,4:T(8,128)S(1)} %get-tuple-element.48) | copy-start | bytes 786436
  121.4 348.4 %copy-start.3 = (f32[256,2,2,64,1,1]{0,3,1,2,5,4:T(8,128)}, f32[256,2,2,64,1,1]{0,3,1,2,5,4:T(8,128)S(1)}, u32[]{:S(2)}) copy-start(f32[256,2,2,64,1,1]{0,3,1,2,5,4:T(8,128)S(1)} %get-tuple-element.47) | copy-start | bytes 786436
  333.8 9.2 slice-start
  333.8 9.2 slice-start.1
  354.8 97.5 %all-to-all-start.1 = ((f32[1,16,256,2,128]{4,1,3,0,2:T(8,128)}), f32[1,16,256,2,128]{4,1,3,0,2:T(8,128)}, u32[]{:S(2)}, u32[]{:S(2)}) async-start(f32[1,16,256,2,128]{4,1,3,0,2:T(8,128)} %copy.54), calls=%async_computation.1 | async-start | bytes 8388608 | tf_op jit(solution)/shard_map/all_to_all | solution.py:140
  469.9 48.5 %copy-start.7 = (f32[16]{0:T(128)S(1)}, f32[16]{0:T(128)}, u32[]{:S(2)}) copy-start(f32[16]{0:T(128)} %param.9) | copy-start | bytes 196
  894.9 8.3 slice-start.2
  894.9 12.1 %copy-start.2 = (f32[256,2,2,64,1]{0,3,1,2,4:T(8,128)S(1)}, f32[256,2,2,64,1]{0,3,1,2,4:T(8,128)}, u32[]{:S(2)}) copy-start(f32[256,2,2,64,1]{0,3,1,2,4:T(8,128)} %copy-done.1) | copy-start | bytes 786436
  894.9 8.3 slice-start.3
  915.0 148.9 %all-to-all-start.3 = ((f32[1,16,256,2,128]{4,1,3,0,2:T(8,128)}), f32[1,16,256,2,128]{4,1,3,0,2:T(8,128)}, u32[]{:S(2)}, u32[]{:S(2)}) async-start(f32[1,16,256,2,128]{4,1,3,0,2:T(8,128)} %copy.67), calls=%async_computation.3 | async-start | bytes 8388608 | tf_op jit(solution)/shard_map/all_to_all | solution.py:156
  1032.8 22.4 %copy-start.5 = (f32[64,128,16]{1,0,2:T(8,128)S(1)}, f32[64,128,16]{1,0,2:T(8,128)}, u32[]{:S(2)}) copy-start(f32[64,128,16]{1,0,2:T(8,128)} %get-tuple-element.43) | copy-start | bytes 1572868
  1032.8 22.4 %copy-start.6 = (f32[64,128,16]{1,0,2:T(8,128)S(1)}, f32[64,128,16]{1,0,2:T(8,128)}, u32[]{:S(2)}) copy-start(f32[64,128,16]{1,0,2:T(8,128)} %get-tuple-element.46) | copy-start | bytes 1572868
  1063.8 17.5 %copy-start.4 = (f32[256,2,2,64,1,1]{0,3,1,2,5,4:T(8,128)S(1)}, f32[256,2,2,64,1,1]{0,3,1,2,5,4:T(8,128)}, u32[]{:S(2)}) copy-start(f32[256,2,2,64,1,1]{0,3,1,2,5,4:T(8,128)} %copy-done.3) | copy-start | bytes 786436
where the time goes:
time: 1160 us; the launch traced here: 1150 us
  local copies, waits for them, and re-layouts  468 us (40%)
  matrix products  283 us (24%)
  blocking collectives  175 us (15%)
  waiting for transfers between devices  163 us (14%)
  other arithmetic  46.8 us (4%)
  starting transfers between devices  16.5 us (1%)
    unnamed x29, local copies, waits for them, and re-layouts  222 us
    all_to_all x1, blocking collectives, body(): lax.all_to_all(grad_spec, 'space', split_axis=4, concat_axis=2, tiled=True)  97.6 us
    all_to_all x1, waiting for transfers between devices, body(): lax.all_to_all(spectrum, 'space', split_axis=4, concat_axis=2, tiled=True)  92.5 us
    reshape x2, local copies, waits for them, and re-layouts, analyse_slab(): return result.reshape(rshape[:4] + (rshape[4] * rshape[5],))  90 us
    dot_general x2, matrix products, restore_slab(): jnp.einsum('bcxrqk,ysrq->bcxysk', split_values, y_table, precision=PRECISE)  80.7 us
    dot_general x3, matrix products, contract(): return jnp.einsum(form, left, right, preferred_element_type=jnp.float32)  78.8 us
    psum x1, blocking collectives, body(): point_total, bias_total = lax.psum((point_sum, bias_sum), 'space')  77.6 us
    dot_general x2, matrix products, restore_slab(): return jnp.dot(rounded, z_table.T, preferred_element_type=jnp.float32)  74.1 us
  transfers between devices with their start and end apart: 3, of which 2 were waited for; matrix products, arithmetic and copies ran while one was open for 8% of the time, Pallas kernels for 0%

commit v1 on v0

--- a/solution.py
+++ b/solution.py
@@ -1,8 +1,11 @@
 import math
 
 import jax
+import numpy as np
 import jax.numpy as jnp
 from jax import lax
+from jax.experimental import pallas as pl
+from jax.experimental.pallas import tpu as pltpu
 from jax.sharding import PartitionSpec as P
 
 MODES = 32
@@ -121,7 +124,7 @@
     return jnp.stack([part_real, part_imag], axis=0)
 
 
-def body(field, cotangent, spectral_weight, point_weight, bias):
+def general_body(field, cotangent, spectral_weight, point_weight, bias):
     spaces = lax.axis_size("space")
     planes = field.shape[2]
     cells_y = field.shape[3]
@@ -161,6 +164,439 @@
     return (activation, grad_field, grad_spectral, point_total * factor, bias_total * factor)
 
 
+CHUNKS = 2
+GROUP = 4
+ROWS = 16
+VMEM = 56 * 1024 * 1024
+BF16 = jnp.bfloat16
+F32 = jnp.float32
+
+
+def np_twiddle(length, frequencies):
+    phase = (np.arange(length)[:, None] * frequencies[None, :] % length) * (TURN / length)
+    factor = 1.0 / math.sqrt(length)
+    return np.cos(phase) * factor, -np.sin(phase) * factor
+
+
+def np_block(length, modes):
+    kept = np.concatenate([np.arange(modes), np.arange(length - modes, length)])
+    real, imag = np_twiddle(length, kept)
+    return np.stack([np.stack([real, imag], 1), np.stack([-imag, real], 1)], 1)
+
+
+def blocked_tables(cells_x, cells_y, cells_z, spaces, chunks):
+    z_real, z_imag = np_twiddle(cells_z, np.arange(MODES))
+    forward_z = np.stack([z_real, z_imag], 1)
+    doubling = np.where(np.arange(MODES) == 0, 1.0, 2.0)
+    double_z = forward_z * doubling
+    eye = np.eye(GROUP)
+
+    def z_down(table):
+        out = np.einsum("zrk,ab->azrbk", table, eye)
+        return out.reshape(GROUP * cells_z, 2 * GROUP * MODES).astype(BF16)
+
+    full_y = np_block(cells_y, MODES)
+    y_split = full_y.reshape(cells_y, 2, 2, spaces, 2 * MODES // spaces)
+    y_down = y_split.transpose(3, 2, 4, 1, 0).reshape(4 * MODES, 2 * cells_y).astype(BF16)
+    y_up = y_split.transpose(1, 0, 3, 2, 4).reshape(2 * cells_y, 4 * MODES).astype(BF16)
+    full_x = np_block(cells_x, MODES)
+    x_split = full_x.reshape(spaces, chunks, cells_x // spaces // chunks, 2, 2, 2 * MODES)
+    x_split = x_split.transpose(1, 0, 2, 3, 4, 5).reshape(cells_x, 2, 2, 2 * MODES)
+    x_down = x_split.transpose(2, 3, 1, 0).reshape(4 * MODES, 2 * cells_x).astype(np.float32)
+    x_up = x_split.transpose(1, 0, 2, 3).reshape(2 * cells_x, 4 * MODES).astype(np.float32)
+    forward, double = z_down(forward_z), z_down(double_z)
+    return forward, double, forward.T.copy(), double.T.copy(), y_down, y_up, x_down, x_up
+
+
+def dot(left, right):
+    return jnp.dot(left, right, preferred_element_type=F32)
+
+
+def dot_exact(left, right):
+    return jnp.dot(left, right, preferred_element_type=F32, precision=PRECISE)
+
+
+def params():
+    return pltpu.CompilerParams(vmem_limit_bytes=VMEM)
+
+
+def fixed(shape):
+    return pl.BlockSpec(shape, lambda *_: (0,) * len(shape))
+
+
+def analyse_planes(planes, z_table, y_table):
+    spectrum = dot(jnp.concatenate(planes, axis=1), z_table).astype(BF16)
+    half = spectrum.shape[1] // 2
+    stacked = jnp.concatenate([spectrum[:, :half], spectrum[:, half:]], axis=0)
+    return dot(y_table, stacked)
+
+
+def analyse_kernel(field, z_table, y_table, wire):
+    count = field.shape[1]
+    for place in range(count):
+        planes = [field[c, place] for c in range(GROUP)]
+        coded = analyse_planes(planes, z_table[...], y_table[...])
+        wire[:, 0, place * 8 : place * 8 + 8, :] = coded.reshape(wire.shape[0], 8, 128)
+
+
+def analyse_call(field, z_table, y_table, spaces, chunk):
+    channels, planes, cells_y, cells_z = field.shape
+    part = planes // CHUNKS
+    step = min(4, part)
+    return pl.pallas_call(
+        analyse_kernel,
+        grid=(channels // GROUP, part // step),
+        in_specs=[
+            pl.BlockSpec(
+                (GROUP, step, cells_y, cells_z),
+                lambda g, x: (g, chunk * (part // step) + x, 0, 0),
+            ),
+            fixed(z_table.shape),
+            fixed(y_table.shape),
+        ],
+        out_specs=pl.BlockSpec((spaces, 1, step * 8, 128), lambda g, x: (0, g, x, 0)),
+        out_shape=jax.ShapeDtypeStruct((spaces, channels // GROUP, part * 8, 128), F32),
+        compiler_params=params(),
+        name="analyse",
+    )(field, z_table, y_table)
+
+
+def lane_swap(blocks):
+    return [
+        jnp.concatenate([b[:, k * MODES : (k + 1) * MODES] for b in blocks], axis=1)
+        for k in range(GROUP)
+    ]
+
+
+def gather_modes(wires, x_table, spectrum):
+    spaces, groups, rows, _ = wires[0].shape
+    part = rows // 8
+
+    def one_group(group, carry):
+        blocks = []
+        for k in range(GROUP):
+            pieces = []
+            for r in range(2):
+                for wire in wires:
+                    for source in range(spaces):
+                        pieces.append(wire[source, group, pl.ds(r * GROUP + k, part, stride=8), :])
+            blocks.append(dot_exact(x_table[...], jnp.concatenate(pieces, axis=0)))
+        for c, block in enumerate(lane_swap(blocks)):
+            spectrum[group * GROUP + c] = block.astype(BF16).astype(F32)
+        return carry
+
+    lax.fori_loop(0, groups, one_group, 0)
+
+
+def scatter_modes(mixed, x_table, wires):
+    spaces, _, rows, _ = wires[0].shape
+    part = rows // 8
+    for k, block in enumerate(lane_swap([mixed[c] for c in range(GROUP)])):
+        result = dot_exact(x_table[...], block)
+        place = 0
+        for s in range(2):
+            for wire in wires:
+                for target in range(spaces):
+                    wire[target, 0, pl.ds(s * GROUP + k, part, stride=8), :] = result[
+                        place : place + part
+                    ]
+                    place += part
+
+
+def mix_kernel(*refs):
+    wires = refs[:CHUNKS]
+    weight, x_down, x_up = refs[CHUNKS : CHUNKS + 3]
+    outs = refs[CHUNKS + 3 : 2 * CHUNKS + 3]
+    kept, spectrum, mixed = refs[2 * CHUNKS + 3 :]
+    step = pl.program_id(0)
+    channels = spectrum.shape[0]
+    half = spectrum.shape[1] // 2
+
+    @pl.when(step == 0)
+    def _():
+        gather_modes(wires, x_down, spectrum)
+        kept[...] = spectrum[...].astype(BF16)
+
+    real = jnp.zeros((half, 128), F32)
+    imag = jnp.zeros((half, 128), F32)
+    for i in range(channels):
+        u_real, u_imag = spectrum[i, :half], spectrum[i, half:]
+        w_real, w_imag = weight[0, i, 0].astype(F32), weight[1, i, 0].astype(F32)
+        real += u_real * w_real - u_imag * w_imag
+        imag += u_real * w_imag + u_imag * w_real
+    place = lax.rem(step, GROUP)
+    mixed[place, :half] = real
+    mixed[place, half:] = imag
+
+    @pl.when(place == GROUP - 1)
+    def _():
+        scatter_modes(mixed, x_up, outs)
+
+
+def dual_kernel(*refs):
+    wires = refs[:CHUNKS]
+    weight, kept, x_down, x_up = refs[CHUNKS : CHUNKS + 4]
+    outs = refs[CHUNKS + 4 : 2 * CHUNKS + 4]
+    slope, spectrum, mixed = refs[2 * CHUNKS + 4 :]
+    step = pl.program_id(0)
+    channels = spectrum.shape[0]
+    half = spectrum.shape[1] // 2
+
+    @pl.when(step == 0)
+    def _():
+        gather_modes(wires, x_down, spectrum)
+
+    u_real, u_imag = kept[0, :half].astype(F32), kept[0, half:].astype(F32)
+    real = jnp.zeros((half, 128), F32)
+    imag = jnp.zeros((half, 128), F32)
+    for o in range(channels):
+        g_real, g_imag = spectrum[o, :half], spectrum[o, half:]
+        w_real, w_imag = weight[0, 0, o].astype(F32), weight[1, 0, o].astype(F32)
+        real += w_real * g_real + w_imag * g_imag
+        imag += w_real * g_imag - w_imag * g_real
+        slope[0, 0, o] = u_real * g_real + u_imag * g_imag
+        slope[1, 0, o] = u_real * g_imag - u_imag * g_real
+    place = lax.rem(step, GROUP)
+    mixed[place, :half] = real
+    mixed[place, half:] = imag
+
+    @pl.when(place == GROUP - 1)
+    def _():
+        scatter_modes(mixed, x_up, outs)
+
+
+def mix_call(wires, weight, kept, x_down, x_up):
+    _, channels, _, modes_x, modes = weight.shape
+    shape = wires[0].shape
+    wire_block = (shape[0], 1) + shape[2:]
+    wire_specs = [fixed(shape) for _ in wires]
+    tables = [fixed(x_down.shape), fixed(x_up.shape)]
+    out_wires = [pl.BlockSpec(wire_block, lambda s: (0, s // GROUP, 0, 0)) for _ in wires]
+    out_shapes = [jax.ShapeDtypeStruct(shape, F32) for _ in wires]
+    scratch = [
+        pltpu.VMEM((channels, 2 * modes_x, modes), F32),
+        pltpu.VMEM((GROUP, 2 * modes_x, modes), F32),
+    ]
+    if kept is None:
+        block = (2, channels, 1, modes_x, modes)
+        return pl.pallas_call(
+            mix_kernel,
+            grid=(channels,),
+            in_specs=wire_specs + [pl.BlockSpec(block, lambda s: (0, 0, s, 0, 0))] + tables,
+            out_specs=out_wires + [fixed((channels, 2 * modes_x, modes))],
+            out_shape=out_shapes + [jax.ShapeDtypeStruct((channels, 2 * modes_x, modes), BF16)],
+            scratch_shapes=scratch,
+            compiler_params=params(),
+            name="mix",
+        )(*wires, weight, x_down, x_up)
+    block = (2, 1, channels, modes_x, modes)
+    return pl.pallas_call(
+        dual_kernel,
+        grid=(channels,),
+        in_specs=wire_specs
+        + [
+            pl.BlockSpec(block, lambda s: (0, s, 0, 0, 0)),
+            pl.BlockSpec((1, 2 * modes_x, modes), lambda s: (s, 0, 0)),
+        ]
+        + tables,
+        out_specs=out_wires + [pl.BlockSpec(block, lambda s: (0, s, 0, 0, 0))],
+        out_shape=out_shapes
+        + [jax.ShapeDtypeStruct((2, channels, channels, modes_x, modes), F32)],
+        scratch_shapes=scratch,
+        compiler_params=params(),
+        name="dual",
+    )(*wires, weight, kept, x_down, x_up)
+
+
+def restore_planes(wire, y_table, z_table, spectral):
+    spaces, groups = wire.shape[:2]
+    cells_y = spectral.shape[1]
+    for g in range(groups):
+        coded = wire[:, g].reshape(spaces * 8, 128).astype(BF16)
+        lines = dot(y_table[...], coded).astype(BF16)
+        lines = jnp.concatenate([lines[:cells_y], lines[cells_y:]], axis=1)
+        planes = dot(lines, z_table[...])
+        for c in range(GROUP):
+            spectral[g * GROUP + c] = planes[:, c * 128 : (c + 1) * 128]
+
+
+def synthesise_kernel(
+    wire, field, cotangent, point, bias, y_up, z_up, z_down, y_down, *refs
+):
+    activation, grad, wire_out, point_sum, bias_sum, spectral = refs[-6:]
+    step = pl.program_id(0)
+    channels, _, cells_y, cells_z = field.shape
+
+    @pl.when(step == 0)
+    def _():
+        point_sum[...] = jnp.zeros_like(point_sum)
+        bias_sum[...] = jnp.zeros_like(bias_sum)
+
+    restore_planes(wire, y_up, z_up, spectral)
+    for row in range(cells_y // ROWS):
+        lines = pl.ds(row * ROWS, ROWS)
+        inputs = field[:, 0, lines, :].reshape(channels * ROWS, cells_z)
+        preact = dot(point[...], inputs)
+        preact += spectral[:, lines, :].reshape(channels * ROWS, cells_z) + bias[...]
+        square = preact * preact
+        tangent = jnp.tanh(preact * (GELU_SCALE + (GELU_SCALE * GELU_CUBE) * square))
+        upper = 0.5 + 0.5 * tangent
+        activation[:, 0, lines, :] = (
+            (preact * upper).astype(BF16).reshape(channels, ROWS, cells_z)
+        )
+        inner = GELU_SCALE + (3.0 * GELU_SCALE * GELU_CUBE) * square
+        slope = upper + (preact * inner) * (0.5 - 0.5 * tangent * tangent)
+        coming = cotangent[:, 0, lines, :].reshape(channels * ROWS, cells_z).astype(F32)
+        low = (coming * slope).astype(BF16)
+        grad[:, 0, lines, :] = low.reshape(channels, ROWS, cells_z)
+        bias_sum[...] += low.astype(F32)
+
+    def by_rows(ref):
+        return jnp.concatenate(
+            [
+                ref[:, 0, row * ROWS : (row + 1) * ROWS, :].reshape(channels * ROWS, cells_z)
+                for row in range(cells_y // ROWS)
+            ],
+            axis=1,
+        )
+
+    point_sum[...] += lax.dot_general(
+        by_rows(field), by_rows(grad), (((1,), (1,)), ((), ())), preferred_element_type=F32
+    )
+    for g in range(channels // GROUP):
+        planes = [grad[g * GROUP + c, 0] for c in range(GROUP)]
+        coded = analyse_planes(planes, z_down[...], y_down[...])
+        wire_out[:, g] = coded.reshape(wire_out.shape[0], 8, 128)
+
+
+def synthesise_call(wire, field, cotangent, point, bias, tables, chunk, earlier):
+    channels, planes, cells_y, cells_z = field.shape
+    part = planes // CHUNKS
+    spaces, groups = wire.shape[:2]
+    slab = pl.BlockSpec((channels, 1, cells_y, cells_z), lambda x: (0, chunk * part + x, 0, 0))
+    wire_spec = pl.BlockSpec((spaces, groups, 8, 128), lambda x: (0, 0, x, 0))
+    side = channels * ROWS
+    operands = [wire, field, cotangent, point, bias] + list(tables)
+    specs = [wire_spec, slab, slab] + [fixed(a.shape) for a in operands[3:]]
+    aliases = {}
+    for index, value in enumerate(earlier):
+        aliases[len(operands)] = index
+        operands.append(value)
+        specs.append(pl.BlockSpec(memory_space=pl.ANY))
+    return pl.pallas_call(
+        synthesise_kernel,
+        grid=(part,),
+        in_specs=specs,
+        out_specs=[slab, slab, wire_spec, fixed((side, side)), fixed((side, cells_z))],
+        out_shape=[
+            jax.ShapeDtypeStruct(field.shape, BF16),
+            jax.ShapeDtypeStruct(field.shape, BF16),
+            jax.ShapeDtypeStruct(wire.shape, F32),
+            jax.ShapeDtypeStruct((side, side), F32),
+            jax.ShapeDtypeStruct((side, cells_z), F32),
+        ],
+        scratch_shapes=[pltpu.VMEM((channels, cells_y, cells_z), F32)],
+        input_output_aliases=aliases,
+        compiler_params=params(),
+        name="synthesise",
+    )(*operands)
+
+
+def finish_kernel(wire, grad, point, y_up, z_up, *refs):
+    grad_field, spectral = refs[-2:]
+    channels, _, cells_y, cells_z = grad.shape
+    restore_planes(wire, y_up, z_up, spectral)
+    for row in range(cells_y // ROWS):
+        lines = pl.ds(row * ROWS, ROWS)
+        inputs = grad[:, 0, lines, :].reshape(channels * ROWS, cells_z)
+        total = dot(point[...], inputs) + spectral[:, lines, :].reshape(channels * ROWS, cells_z)
+        grad_field[:, 0, lines, :] = total.astype(BF16).reshape(channels, ROWS, cells_z)
+
+
+def finish_call(wire, grad, point, y_up, z_up, chunk, earlier):
+    channels, planes, cells_y, cells_z = grad.shape
+    part = planes // CHUNKS
+    spaces, groups = wire.shape[:2]
+    slab = pl.BlockSpec((channels, 1, cells_y, cells_z), lambda x: (0, chunk * part + x, 0, 0))
+    operands = [wire, grad, point, y_up, z_up]
+    specs = [pl.BlockSpec((spaces, groups, 8, 128), lambda x: (0, 0, x, 0)), slab]
+    specs += [fixed(a.shape) for a in operands[2:]]
+    aliases = {}
+    for value in earlier:
+        aliases[len(operands)] = 0
+        operands.append(value)
+        specs.append(pl.BlockSpec(memory_space=pl.ANY))
+    return pl.pallas_call(
+        finish_kernel,
+        grid=(part,),
+        in_specs=specs,
+        out_specs=slab,
+        out_shape=jax.ShapeDtypeStruct(grad.shape, BF16),
+        scratch_shapes=[pltpu.VMEM((channels, cells_y, cells_z), F32)],
+        input_output_aliases=aliases,
+        compiler_params=params(),
+        name="finish",
+    )(*operands)
+
+
+def exchange(values):
+    return lax.all_to_all(values, "space", split_axis=0, concat_axis=0, tiled=True)
+
+
+def blocked_body(field, cotangent, spectral_weight, point_weight, bias):
+    spaces = lax.axis_size("space")
+    _, channels, planes, cells_y, cells_z = field.shape
+    cells_x = planes * spaces
+    tables = blocked_tables(cells_x, cells_y, cells_z, spaces, CHUNKS)
+    z_down, z_down2, z_up, z_up2, y_down, y_up, x_down, x_up = map(jnp.asarray, tables)
+    field_part, cotangent_part = field[0], cotangent[0]
+    eye = jnp.eye(ROWS, dtype=F32)
+    point_in = jnp.kron(point_weight.T.astype(F32), eye).astype(BF16)
+    point_out = jnp.kron(point_weight.astype(F32), eye).astype(BF16)
+    bias_rows = jnp.broadcast_to(jnp.repeat(bias, ROWS)[:, None], (channels * ROWS, cells_z))
+    chunks = range(CHUNKS)
+    wires = [exchange(analyse_call(field_part, z_down, y_down, spaces, h)) for h in chunks]
+    *wires, kept = mix_call(wires, spectral_weight, None, x_down, x_up)
+    wires = [exchange(w) for w in wires]
+    earlier, back, point_sums, bias_sums = [], [], 0.0, 0.0
+    for h in chunks:
+        activation, grad, wire, point_sum, bias_sum = synthesise_call(
+            wires[h], field_part, cotangent_part, point_in, bias_rows,
+            (y_up, z_up2, z_down2, y_down), h, earlier,
+        )
+        earlier = [activation, grad]
+        back.append(exchange(wire))
+        point_sums, bias_sums = point_sums + point_sum, bias_sums + bias_sum
+    point_part = jnp.sum(
+        point_sums.reshape(channels, ROWS, channels, ROWS) * eye[None, :, None, :], axis=(1, 3)
+    )
+    bias_part = jnp.sum(bias_sums.reshape(channels, -1), axis=1)
+    *wires, grad_spectral = mix_call(back, spectral_weight, kept, x_down, x_up)
+    wires = [exchange(w) for w in wires]
+    point_total, bias_total = lax.psum((point_part, bias_part), "space")
+    finished = []
+    for h in chunks:
+        finished = [finish_call(wires[h], grad, point_out, y_up, z_up, h, finished)]
+    factor = 1.0 / math.sqrt(cells_x * cells_y * cells_z)
+    return (
+        activation[None],
+        finished[0][None],
+        grad_spectral,
+        point_total * factor,
+        bias_total * factor,
+    )
+
+
+def body(field, cotangent, spectral_weight, point_weight, bias):
+    blocked = (
+        field.shape == (1, 16, 16, 256, 128)
+        and spectral_weight.shape == (2, 16, 16, 64, 128)
+        and lax.axis_size("space") == 16
+    )
+    chosen = blocked_body if blocked else general_body
+    return chosen(field, cotangent, spectral_weight, point_weight, bias)
+
+
 def solution(mesh):
     placed = (
         P("groups", None, "space", None, None),

time: 1160 us -> 541 us (0.47)
  local copies, waits for them, and re-layouts: 468 us -> 8.99 us
  matrix products: 283 us -> 0 us
  Pallas kernels: 0 us -> 176 us
  waiting for transfers between devices: 163 us -> 59 us
  blocking collectives: 175 us -> 271 us
  other arithmetic: 46.8 us -> 3.59 us
    dot_general x15 -> x0, matrix products: 283 us -> none  [the longest x2 80.7 us: restore_slab(): jnp.einsum('bcxrqk,ysrq->bcxysk', split_values, y_table, precision=PRECISE)]
    unnamed x29 -> x18, local copies, waits for them, and re-layouts: 222 us -> 2.67 us
    pallas_call x0 -> x8, Pallas kernels: none -> 176 us  [the longest x2 68.8 us: synthesise_call(): pl.pallas_call(synthesise_kernel, grid=(part,), in_specs=specs, out_specs...]
    all_to_all x1 -> x4, blocking collectives: 97.6 us -> 210 us  [exchange(): lax.all_to_all(values, 'space', split_axis=0, concat_axis=0, tiled=True)]
    all_to_all x7 -> x0, local copies, waits for them, and re-layouts: 109 us -> none  [the longest x3 48.4 us: body(): lax.all_to_all(spectrum, 'space', split_axis=4, concat_axis=2, tiled=True)]
    all_to_all x3 -> x4, waiting for transfers between devices: 163 us -> 59 us  [exchange(): lax.all_to_all(values, 'space', split_axis=0, concat_axis=0, tiled=True)]
    reshape x2 -> x1, local copies, waits for them, and re-layouts: 90 us -> 1.98 us  [blocked_body(): point_sums.reshape(channels, ROWS, channels, ROWS) * eye[None, :, None, :]]
    all_to_all x2 -> x0, other arithmetic: 28 us -> none  [the longest x1 14 us: body(): lax.all_to_all(grad_spec, 'space', split_axis=4, concat_axis=2, tiled=True)]
  transfers between devices with their start and end apart: 3 -> 4, of which waited for: 2 -> 3; matrix products, arithmetic and copies ran while one was open for 8% -> 2% of each run, Pallas kernels for 0% -> 18%
where the time goes in v1:
time: 541 us; the launch traced here: 539 us
  blocking collectives  271 us (50%)
  Pallas kernels  176 us (33%)
  waiting for transfers between devices  59 us (11%)
  starting transfers between devices  20.8 us (4%)
  local copies, waits for them, and re-layouts  8.99 us (2%)
    all_to_all x4, blocking collectives, exchange(): lax.all_to_all(values, 'space', split_axis=0, concat_axis=0, tiled=True)  210 us
    pallas_call x2, Pallas kernels, synthesise_call(): pl.pallas_call(synthesise_kernel, grid=(part,), in_specs=specs, out_specs...  68.8 us
    psum x1, blocking collectives, blocked_body(): point_total, bias_total = lax.psum((point_part, bias_part), 'space')  60.7 us
    all_to_all x4, waiting for transfers between devices, exchange(): lax.all_to_all(values, 'space', split_axis=0, concat_axis=0, tiled=True)  59 us
    pallas_call x2, Pallas kernels, finish_call(): pl.pallas_call(finish_kernel, grid=(part,), in_specs=specs, out_specs=sla...  31.5 us
    pallas_call x1, Pallas kernels, mix_call(): pl.pallas_call(dual_kernel, grid=(channels,), in_specs=wire_specs + [pl.B...  26.5 us
    pallas_call x2, Pallas kernels, analyse_call(): pl.pallas_call(analyse_kernel, grid=(channels // GROUP, part // step), in...  24.7 us
    pallas_call x1, Pallas kernels, mix_call(): pl.pallas_call(mix_kernel, grid=(channels,), in_specs=wire_specs + [pl.Bl...  24.2 us
  transfers between devices with their start and end apart: 4, of which 3 were waited for; matrix products, arithmetic and copies ran while one was open for 2% of the time, Pallas kernels for 18%

profile of v1, /device:TPU:16, one launch (start us, length us, event | category | flops | bytes accessed | tf_op | source)
XLA Modules:
  0.0 539.2 jit_solution(17485468971936307222)
XLA Ops:
  0.6 12.3 %analyse.3 = f32[16,4,64,128]{3,2,1,0:T(8,128)} custom-call(bf16[16,16,256,128]{3,2,1,0:T(8,128)(2,1)} %bitcast.10, bf16[512,256]{1,0:T(8,128)(2,1)} %constant.9.clone.z_table, bf16[128,512]{1,0:T(8,128)(2,1)} %constant.25.clone.y_table.y_down), custom_call_target="tpu_custom_call" | custom-call | tf_op jit(solution)/shard_map/analyse/pallas_call | solution.py:246
  13.0 6.2 %all-to-all-start.1 = ((f32[16,4,64,128]{3,2,1,0:T(8,128)}), f32[16,4,64,128]{3,2,1,0:T(8,128)S(1)}, u32[]{:S(2)}, u32[]{:S(2)}) async-start(f32[16,4,64,128]{3,2,1,0:T(8,128)} %analyse.3), calls=%async_computation.1 | async-start | bytes 4194304 | tf_op jit(solution)/shard_map/all_to_all | solution.py:543
  19.1 12.3 %analyse.2 = f32[16,4,64,128]{3,2,1,0:T(8,128)} custom-call(bf16[16,16,256,128]{3,2,1,0:T(8,128)(2,1)} %bitcast.11, bf16[512,256]{1,0:T(8,128)(2,1)} %constant.9.clone.z_table, bf16[128,512]{1,0:T(8,128)(2,1)} %constant.25.clone.y_table.y_down), custom_call_target="tpu_custom_call" | custom-call | tf_op jit(solution)/shard_map/analyse/pallas_call | solution.py:246
  31.5 35.3 %all-to-all-done.1.refs_1_ = f32[16,4,64,128]{3,2,1,0:T(8,128)S(1)} async-done(((f32[16,4,64,128]{3,2,1,0:T(8,128)}), f32[16,4,64,128]{3,2,1,0:T(8,128)S(1)}, u32[]{:S(2)}, u32[]{:S(2)}) %all-to-all-start.1) | async-done | bytes 2097184 | tf_op jit(solution)/shard_map/all_to_all | solution.py:543
  66.8 0.0 copy-start.2
  66.8 52.4 %all_to_all.40.refs_0_ = f32[16,4,64,128]{3,2,1,0:T(8,128)} all-to-all(f32[16,4,64,128]{3,2,1,0:T(8,128)} %analyse.2), channel_id=1, replica_groups=mesh['groups'=2,'space'=16] {'space'}, dimensions={0} | all-to-all | bytes 4194304 | tf_op jit(solution)/shard_map/all_to_all | solution.py:543
  119.2 0.0 copy-done.2
  119.2 24.2 %mix.1 = (f32[16,4,64,128]{3,2,1,0:T(8,128)}, f32[16,4,64,128]{3,2,1,0:T(8,128)}, bf16[16,128,128]{2,1,0:T(8,128)(2,1)}) custom-call(f32[16,4,64,128]{3,2,1,0:T(8,128)} %all_to_all.40.refs_0_, f32[16,4,64,128]{3,2,1,0:T(8,128)} %copy-done.2, bf16[2,16,16,64,128]{4,3,2,1,0:T(8,128)(2,1)} %refs_2_.3, f32[128,512]{1,0:T(8,128)} %constant.27.clone.refs_3_.refs_4_, ...), custom_call_target="tpu_custom_call" | custom-call | tf_op jit(solution)/shard_map/mix/pallas_call | solution.py:382
  143.3 52.5 %all_to_all.41.wire = f32[16,4,64,128]{3,2,1,0:T(8,128)} all-to-all(f32[16,4,64,128]{3,2,1,0:T(8,128)} %get-tuple-element.22), channel_id=1, replica_groups=mesh['groups'=2,'space'=16] {'space'}, dimensions={0} | all-to-all | bytes 4194304 | tf_op jit(solution)/shard_map/all_to_all | solution.py:543
  195.9 0.0 copy-start.8
  195.9 0.0 copy-start.7
  195.9 5.0 all-to-all-start.2
  200.8 0.0 copy-done.8
  200.9 0.1 broadcast_in_dim.23
  200.9 0.1 broadcast_in_dim.24
  201.0 0.0 copy-done.7
  201.0 0.1 copy.22
  201.1 0.2 multiply_convert_fusion.1
  201.3 1.6 convert_element_type.34.point
  203.0 0.7 broadcast_in_dim.25.bias
  203.7 34.4 %synthesise.2 = (bf16[16,16,256,128]{3,2,1,0:T(8,128)(2,1)}, bf16[16,16,256,128]{3,2,1,0:T(8,128)(2,1)}, f32[16,4,64,128]{3,2,1,0:T(8,128)}, f32[256,256]{1,0:T(8,128)}, f32[256,128]{1,0:T(8,128)}) custom-call(f32[16,4,64,128]{3,2,1,0:T(8,128)} %all_to_all.41.wire, bf16[16,16,256,128]{3,2,1,0:T(8,128)(2,1)} %bitcast.12, bf16[16,16,256,128]{3,2,1,0:T(8,128)(2,1)} %bitcast.15, ...), custom_call_target="tpu_custom_call" | custom-call | tf_op jit(solution)/shard_map/synthesise/pallas_call | solution.py:486
  238.1 10.4 %all-to-all-done.2.wire = f32[16,4,64,128]{3,2,1,0:T(8,128)S(1)} async-done(((f32[16,4,64,128]{3,2,1,0:T(8,128)}), f32[16,4,64,128]{3,2,1,0:T(8,128)S(1)}, u32[]{:S(2)}, u32[]{:S(2)}) %all-to-all-start.2) | async-done | bytes 2097184 | tf_op jit(solution)/shard_map/all_to_all | solution.py:543
  248.5 0.0 copy-start.1
  248.5 1.3 copy-done.1
  249.8 4.7 all-to-all-start.4
  254.5 34.4 %synthesise.3 = (bf16[16,16,256,128]{3,2,1,0:T(8,128)(2,1)}, bf16[16,16,256,128]{3,2,1,0:T(8,128)(2,1)}, f32[16,4,64,128]{3,2,1,0:T(8,128)}, f32[256,256]{1,0:T(8,128)}, f32[256,128]{1,0:T(8,128)}) custom-call(f32[16,4,64,128]{3,2,1,0:T(8,128)} %copy-done.1, bf16[16,16,256,128]{3,2,1,0:T(8,128)(2,1)} %bitcast.13, ...), custom_call_target="tpu_custom_call", output_to_operand_aliasing={{0}: (9, {}), {1}: (10, {})} | custom-call | tf_op jit(solution)/shard_map/synthesise/pallas_call | solution.py:486
  288.9 13.3 %all-to-all-done.4.refs_0_ = f32[16,4,64,128]{3,2,1,0:T(8,128)} async-done(((f32[16,4,64,128]{3,2,1,0:T(8,128)}), f32[16,4,64,128]{3,2,1,0:T(8,128)}, u32[]{:S(2)}, u32[]{:S(2)}) %all-to-all-start.4) | async-done | bytes 2097184 | tf_op jit(solution)/shard_map/all_to_all | solution.py:543
  302.2 52.4 %all_to_all.42.refs_1_ = f32[16,4,64,128]{3,2,1,0:T(8,128)} all-to-all(f32[16,4,64,128]{3,2,1,0:T(8,128)} %get-tuple-element.27), channel_id=1, replica_groups=mesh['groups'=2,'space'=16] {'space'}, dimensions={0} | all-to-all | bytes 4194304 | tf_op jit(solution)/shard_map/all_to_all | solution.py:543
  354.6 26.5 %dual.1 = (f32[16,4,64,128]{3,2,1,0:T(8,128)}, f32[16,4,64,128]{3,2,1,0:T(8,128)}, f32[2,16,16,64,128]{4,3,2,1,0:T(8,128)}) custom-call(f32[16,4,64,128]{3,2,1,0:T(8,128)} %all-to-all-done.4.refs_0_, f32[16,4,64,128]{3,2,1,0:T(8,128)} %all_to_all.42.refs_1_, bf16[2,16,16,64,128]{4,3,2,1,0:T(8,128)(2,1)} %refs_2_.3, ...), custom_call_target="tpu_custom_call" | custom-call | tf_op jit(solution)/shard_map/dual/pallas_call | solution.py:393
  381.1 52.5 %all_to_all.43.wire = f32[16,4,64,128]{3,2,1,0:T(8,128)} all-to-all(f32[16,4,64,128]{3,2,1,0:T(8,128)} %get-tuple-element.31), channel_id=1, replica_groups=mesh['groups'=2,'space'=16] {'space'}, dimensions={0} | all-to-all | bytes 4194304 | tf_op jit(solution)/shard_map/all_to_all | solution.py:543
  433.6 5.0 all-to-all-start.6
  438.6 0.0 copy-done.5
  438.6 0.0 copy-done.6
  438.6 0.1 add_reduce_fusion
  438.7 0.1 reduce_sum.27
  438.8 0.0 copy-done.3
  438.8 0.0 copy-done.4
  438.9 2.0 reshape.37
  440.8 2.0 multiply_reduce_fusion
  442.8 1.6 convert_element_type.37.point
  444.4 0.1 reduce_sum.28
  444.6 60.7 %all-reduce = (f32[16,16]{1,0:T(8,128)S(1)}, f32[16]{0:T(128)S(1)}) all-reduce(f32[16,16]{1,0:T(8,128)S(1)} %get-tuple-element.39, f32[16]{0:T(128)S(1)} %reduce_sum.28), channel_id=1, replica_groups=mesh['groups'=2,'space'=16] {'space'}, use_global_device_ids=true, to_apply=%region_1.2 | all-reduce | flops 272 | bytes 2176 | tf_op jit(solution)/shard_map/psum | solution.py:576
  505.3 0.5 broadcast_multiply_fusion.1
  505.8 0.6 broadcast_multiply_fusion
  506.4 15.8 %finish.2.refs_0_ = bf16[16,16,256,128]{3,2,1,0:T(8,128)(2,1)} custom-call(f32[16,4,64,128]{3,2,1,0:T(8,128)} %all_to_all.43.wire, bf16[16,16,256,128]{3,2,1,0:T(8,128)(2,1)} %get-tuple-element.30.grad, bf16[256,256]{1,0:T(8,128)(2,1)} %convert_element_type.37.point, bf16[512,128]{1,0:T(8,128)(2,1)} %constant.26.clone.y_up, bf16[256,512]{1,0:T(8,128)(2,1)} %constant.23.clone.z_up), custom_call_target="tpu_custom_call" | custom-call | tf_op jit(solution)/shard_map/finish/pallas_call | solution.py:529
  522.1 0.0 all-to-all-done.6.wire
  522.1 1.3 copy-done
  523.5 15.8 %finish.3 = bf16[16,16,256,128]{3,2,1,0:T(8,128)(2,1)} custom-call(f32[16,4,64,128]{3,2,1,0:T(8,128)} %copy-done, bf16[16,16,256,128]{3,2,1,0:T(8,128)(2,1)} %get-tuple-element.30.grad, bf16[256,256]{1,0:T(8,128)(2,1)} %convert_element_type.37.point, bf16[512,128]{1,0:T(8,128)(2,1)} %constant.26.clone.y_up, ...), custom_call_target="tpu_custom_call", output_to_operand_aliasing={{}: (5, {})} | custom-call | tf_op jit(solution)/shard_map/finish/pallas_call | solution.py:529
  (8 shorter events, 0.1 us)
Async XLA Ops:
  13.0 53.8 %all-to-all-start.1 = ((f32[16,4,64,128]{3,2,1,0:T(8,128)}), f32[16,4,64,128]{3,2,1,0:T(8,128)S(1)}, u32[]{:S(2)}, u32[]{:S(2)}) async-start(f32[16,4,64,128]{3,2,1,0:T(8,128)} %analyse.3), calls=%async_computation.1 | async-start | bytes 4194304 | tf_op jit(solution)/shard_map/all_to_all | solution.py:543
  66.8 52.4 %copy-start.2 = (f32[16,4,64,128]{3,2,1,0:T(8,128)}, f32[16,4,64,128]{3,2,1,0:T(8,128)S(1)}, u32[]{:S(2)}) copy-start(f32[16,4,64,128]{3,2,1,0:T(8,128)S(1)} %all-to-all-done.1.refs_1_) | copy-start | bytes 6291460
  195.9 5.0 copy-start.8
  195.9 5.1 copy-start.7
  195.9 52.6 %all-to-all-start.2 = ((f32[16,4,64,128]{3,2,1,0:T(8,128)}), f32[16,4,64,128]{3,2,1,0:T(8,128)S(1)}, u32[]{:S(2)}, u32[]{:S(2)}) async-start(f32[16,4,64,128]{3,2,1,0:T(8,128)} %get-tuple-element.21), calls=%async_computation.2 | async-start | bytes 4194304 | tf_op jit(solution)/shard_map/all_to_all | solution.py:543
  248.5 1.3 copy-start.1
  249.8 52.4 %all-to-all-start.4 = ((f32[16,4,64,128]{3,2,1,0:T(8,128)}), f32[16,4,64,128]{3,2,1,0:T(8,128)}, u32[]{:S(2)}, u32[]{:S(2)}) async-start(f32[16,4,64,128]{3,2,1,0:T(8,128)} %get-tuple-element.26), calls=%async_computation.4 | async-start | bytes 4194304 | tf_op jit(solution)/shard_map/all_to_all | solution.py:543
  433.6 5.0 copy-start.5
  433.6 5.0 copy-start.6
  433.6 5.2 copy-start.3
  433.6 5.2 copy-start.4
  433.6 88.5 %all-to-all-start.6 = ((f32[16,4,64,128]{3,2,1,0:T(8,128)}), f32[16,4,64,128]{3,2,1,0:T(8,128)S(1)}, u32[]{:S(2)}, u32[]{:S(2)}) async-start(f32[16,4,64,128]{3,2,1,0:T(8,128)} %get-tuple-element.29), calls=%async_computation.6 | async-start | bytes 4194304 | tf_op jit(solution)/shard_map/all_to_all | solution.py:543
  522.1 1.3 copy-start

commit v2 on v1

--- a/solution.py
+++ b/solution.py
@@ -184,6 +184,12 @@
     return np.stack([np.stack([real, imag], 1), np.stack([-imag, real], 1)], 1)
 
 
+def in_halves(table):
+    high = table.astype(BF16)
+    low = (table - high.astype(np.float64)).astype(BF16)
+    return np.concatenate([high, high, low], axis=1)
+
+
 def blocked_tables(cells_x, cells_y, cells_z, spaces, chunks):
     z_real, z_imag = np_twiddle(cells_z, np.arange(MODES))
     forward_z = np.stack([z_real, z_imag], 1)
@@ -202,18 +208,20 @@
     full_x = np_block(cells_x, MODES)
     x_split = full_x.reshape(spaces, chunks, cells_x // spaces // chunks, 2, 2, 2 * MODES)
     x_split = x_split.transpose(1, 0, 2, 3, 4, 5).reshape(cells_x, 2, 2, 2 * MODES)
-    x_down = x_split.transpose(2, 3, 1, 0).reshape(4 * MODES, 2 * cells_x).astype(np.float32)
-    x_up = x_split.transpose(1, 0, 2, 3).reshape(2 * cells_x, 4 * MODES).astype(np.float32)
+    x_down = x_split.transpose(2, 3, 1, 0).reshape(4 * MODES, 2 * cells_x)
+    x_up = x_split.transpose(1, 0, 2, 3).reshape(2 * cells_x, 4 * MODES)
     forward, double = z_down(forward_z), z_down(double_z)
-    return forward, double, forward.T.copy(), double.T.copy(), y_down, y_up, x_down, x_up
+    return forward, double, forward.T.copy(), double.T.copy(), y_down, y_up, in_halves(x_down), in_halves(x_up)
 
 
 def dot(left, right):
     return jnp.dot(left, right, preferred_element_type=F32)
 
 
-def dot_exact(left, right):
-    return jnp.dot(left, right, preferred_element_type=F32, precision=PRECISE)
+def dot_halves(table, values):
+    high = values.astype(BF16)
+    low = (values - high.astype(F32)).astype(BF16)
+    return dot(table, jnp.concatenate([high, low, high], axis=0))
 
 
 def params():
@@ -280,7 +288,7 @@
                 for wire in wires:
                     for source in range(spaces):
                         pieces.append(wire[source, group, pl.ds(r * GROUP + k, part, stride=8), :])
-            blocks.append(dot_exact(x_table[...], jnp.concatenate(pieces, axis=0)))
+            blocks.append(dot_halves(x_table[...], jnp.concatenate(pieces, axis=0)))
         for c, block in enumerate(lane_swap(blocks)):
             spectrum[group * GROUP + c] = block.astype(BF16).astype(F32)
         return carry
@@ -292,7 +300,7 @@
     spaces, _, rows, _ = wires[0].shape
     part = rows // 8
     for k, block in enumerate(lane_swap([mixed[c] for c in range(GROUP)])):
-        result = dot_exact(x_table[...], block)
+        result = dot_halves(x_table[...], block)
         place = 0
         for s in range(2):
             for wire in wires:
@@ -335,9 +343,9 @@
 
 def dual_kernel(*refs):
     wires = refs[:CHUNKS]
-    weight, kept, x_down, x_up = refs[CHUNKS : CHUNKS + 4]
-    outs = refs[CHUNKS + 4 : 2 * CHUNKS + 4]
-    slope, spectrum, mixed = refs[2 * CHUNKS + 4 :]
+    weight, kept, x_down, x_up, sums = refs[CHUNKS : CHUNKS + 5]
+    outs = refs[CHUNKS + 5 : 2 * CHUNKS + 5]
+    slope, spectrum, mixed = refs[2 * CHUNKS + 5 :]
     step = pl.program_id(0)
     channels = spectrum.shape[0]
     half = spectrum.shape[1] // 2
@@ -363,9 +371,11 @@
     @pl.when(place == GROUP - 1)
     def _():
         scatter_modes(mixed, x_up, outs)
-
-
-def mix_call(wires, weight, kept, x_down, x_up):
+        targets, _, rows, lanes = outs[-1].shape
+        outs[-1][:, 0, rows - 8 :, :] = jnp.broadcast_to(sums[0][None], (targets, 8, lanes))
+
+
+def mix_call(wires, weight, kept, sums, x_down, x_up):
     _, channels, _, modes_x, modes = weight.shape
     shape = wires[0].shape
     wire_block = (shape[0], 1) + shape[2:]
@@ -390,6 +400,10 @@
             name="mix",
         )(*wires, weight, x_down, x_up)
     block = (2, 1, channels, modes_x, modes)
+    longer = shape[2] + 8
+    last_block = (shape[0], 1, longer, shape[3])
+    out_wires[-1] = pl.BlockSpec(last_block, lambda s: (0, s // GROUP, 0, 0))
+    out_shapes[-1] = jax.ShapeDtypeStruct(shape[:2] + (longer, shape[3]), F32)
     return pl.pallas_call(
         dual_kernel,
         grid=(channels,),
@@ -398,14 +412,15 @@
             pl.BlockSpec(block, lambda s: (0, s, 0, 0, 0)),
             pl.BlockSpec((1, 2 * modes_x, modes), lambda s: (s, 0, 0)),
         ]
-        + tables,
+        + tables
+        + [pl.BlockSpec((1, 8, 128), lambda s: (s // GROUP, 0, 0))],
         out_specs=out_wires + [pl.BlockSpec(block, lambda s: (0, s, 0, 0, 0))],
         out_shape=out_shapes
         + [jax.ShapeDtypeStruct((2, channels, channels, modes_x, modes), F32)],
         scratch_shapes=scratch,
         compiler_params=params(),
         name="dual",
-    )(*wires, weight, kept, x_down, x_up)
+    )(*wires, weight, kept, x_down, x_up, sums)
 
 
 def restore_planes(wire, y_table, z_table, spectral):
@@ -556,7 +571,7 @@
     bias_rows = jnp.broadcast_to(jnp.repeat(bias, ROWS)[:, None], (channels * ROWS, cells_z))
     chunks = range(CHUNKS)
     wires = [exchange(analyse_call(field_part, z_down, y_down, spaces, h)) for h in chunks]
-    *wires, kept = mix_call(wires, spectral_weight, None, x_down, x_up)
+    *wires, kept = mix_call(wires, spectral_weight, None, None, x_down, x_up)
     wires = [exchange(w) for w in wires]
     earlier, back, point_sums, bias_sums = [], [], 0.0, 0.0
     for h in chunks:
@@ -571,9 +586,14 @@
         point_sums.reshape(channels, ROWS, channels, ROWS) * eye[None, :, None, :], axis=(1, 3)
     )
     bias_part = jnp.sum(bias_sums.reshape(channels, -1), axis=1)
-    *wires, grad_spectral = mix_call(back, spectral_weight, kept, x_down, x_up)
+    sums = jnp.concatenate([point_part.reshape(-1), bias_part])
+    groups = channels // GROUP
+    padded = jnp.pad(sums, (0, groups * 1024 - sums.shape[0])).reshape(groups, 8, 128)
+    *wires, grad_spectral = mix_call(back, spectral_weight, kept, padded, x_down, x_up)
     wires = [exchange(w) for w in wires]
-    point_total, bias_total = lax.psum((point_part, bias_part), "space")
+    totals = jnp.sum(wires[-1][:, :, -8:, :], axis=0).reshape(-1)
+    point_total = totals[: channels * channels].reshape(channels, channels)
+    bias_total = totals[channels * channels : channels * (channels + 1)]
     finished = []
     for h in chunks:
         finished = [finish_call(wires[h], grad, point_out, y_up, z_up, h, finished)]

time: 541 us -> 504 us (0.932)
  blocking collectives: 271 us -> 157 us
  waiting for transfers between devices: 59 us -> 140 us
  Pallas kernels: 176 us -> 168 us
    all_to_all x4 -> x5, waiting for transfers between devices: 59 us -> 140 us  [exchange(): lax.all_to_all(values, 'space', split_axis=0, concat_axis=0, tiled=True)]
    psum x1 -> x0, blocking collectives: 60.7 us -> none  [blocked_body(): point_total, bias_total = lax.psum((point_part, bias_part), 'space')]
    all_to_all x4 -> x3, blocking collectives: 210 us -> 157 us  [exchange(): lax.all_to_all(values, 'space', split_axis=0, concat_axis=0, tiled=True)]
    all_to_all x4 -> x5, starting transfers between devices: 20.8 us -> 25.5 us  [exchange(): lax.all_to_all(values, 'space', split_axis=0, concat_axis=0, tiled=True)]
  transfers between devices with their start and end apart: 4 -> 5, of which waited for: 3 -> 5; matrix products, arithmetic and copies ran while one was open for 2% -> 1% of each run, Pallas kernels for 18% -> 19%
where the time goes in v2:
time: 504 us; the launch traced here: 502 us
  Pallas kernels  168 us (33%)
  blocking collectives  157 us (31%)
  waiting for transfers between devices  140 us (28%)
  starting transfers between devices  25.5 us (5%)
  local copies, waits for them, and re-layouts  6.56 us (1%)
    all_to_all x3, blocking collectives, exchange(): lax.all_to_all(values, 'space', split_axis=0, concat_axis=0, tiled=True)  157 us
    all_to_all x5, waiting for transfers between devices, exchange(): lax.all_to_all(values, 'space', split_axis=0, concat_axis=0, tiled=True)  140 us
    pallas_call x2, Pallas kernels, synthesise_call(): pl.pallas_call(synthesise_kernel, grid=(part,), in_specs=specs, out_specs...  68.8 us
    pallas_call x2, Pallas kernels, finish_call(): pl.pallas_call(finish_kernel, grid=(part,), in_specs=specs, out_specs=sla...  31.5 us
    all_to_all x5, starting transfers between devices, exchange(): lax.all_to_all(values, 'space', split_axis=0, concat_axis=0, tiled=True)  25.5 us
    pallas_call x2, Pallas kernels, analyse_call(): pl.pallas_call(analyse_kernel, grid=(channels // GROUP, part // step), in...  24.7 us
    pallas_call x1, Pallas kernels, mix_call(): pl.pallas_call(dual_kernel, grid=(channels,), in_specs=wire_specs + [pl.B...  22.9 us
    pallas_call x1, Pallas kernels, mix_call(): pl.pallas_call(mix_kernel, grid=(channels,), in_specs=wire_specs + [pl.Bl...  20.6 us
  transfers between devices with their start and end apart: 5, of which 5 were waited for; matrix products, arithmetic and copies ran while one was open for 1% of the time, Pallas kernels for 19%

profile of v2, /device:TPU:16, one launch (start us, length us, event | category | flops | bytes accessed | tf_op | source)
XLA Modules:
  0.0 501.7 jit_solution(17184250746670437620)
XLA Ops:
  0.6 12.3 %analyse.2 = f32[16,4,64,128]{3,2,1,0:T(8,128)} custom-call(bf16[16,16,256,128]{3,2,1,0:T(8,128)(2,1)} %bitcast.13, bf16[512,256]{1,0:T(8,128)(2,1)} %constant.9.clone.z_table, bf16[128,512]{1,0:T(8,128)(2,1)} %constant.27.clone.y_table.y_down), custom_call_target="tpu_custom_call" | custom-call | tf_op jit(solution)/shard_map/analyse/pallas_call | solution.py:254
  13.0 6.2 %all-to-all-start = ((f32[16,4,64,128]{3,2,1,0:T(8,128)}), f32[16,4,64,128]{3,2,1,0:T(8,128)S(1)}, u32[]{:S(2)}, u32[]{:S(2)}) async-start(f32[16,4,64,128]{3,2,1,0:T(8,128)} %analyse.2), calls=%async_computation | async-start | bytes 4194304 | tf_op jit(solution)/shard_map/all_to_all | solution.py:558
  19.1 12.3 %analyse.3 = f32[16,4,64,128]{3,2,1,0:T(8,128)} custom-call(bf16[16,16,256,128]{3,2,1,0:T(8,128)(2,1)} %bitcast.14, bf16[512,256]{1,0:T(8,128)(2,1)} %constant.9.clone.z_table, bf16[128,512]{1,0:T(8,128)(2,1)} %constant.27.clone.y_table.y_down), custom_call_target="tpu_custom_call" | custom-call | tf_op jit(solution)/shard_map/analyse/pallas_call | solution.py:254
  31.4 35.3 %all-to-all-done.refs_0_ = f32[16,4,64,128]{3,2,1,0:T(8,128)S(1)} async-done(((f32[16,4,64,128]{3,2,1,0:T(8,128)}), f32[16,4,64,128]{3,2,1,0:T(8,128)S(1)}, u32[]{:S(2)}, u32[]{:S(2)}) %all-to-all-start) | async-done | bytes 2097184 | tf_op jit(solution)/shard_map/all_to_all | solution.py:558
  66.8 52.4 %all_to_all.40.refs_1_ = f32[16,4,64,128]{3,2,1,0:T(8,128)} all-to-all(f32[16,4,64,128]{3,2,1,0:T(8,128)} %analyse.3), channel_id=1, replica_groups=mesh['groups'=2,'space'=16] {'space'}, dimensions={0} | all-to-all | bytes 4194304 | tf_op jit(solution)/shard_map/all_to_all | solution.py:558
  119.1 0.0 copy-done.2
  119.2 20.6 %mix.1 = (f32[16,4,64,128]{3,2,1,0:T(8,128)}, f32[16,4,64,128]{3,2,1,0:T(8,128)}, bf16[16,128,128]{2,1,0:T(8,128)(2,1)}) custom-call(f32[16,4,64,128]{3,2,1,0:T(8,128)} %copy-done.2, f32[16,4,64,128]{3,2,1,0:T(8,128)} %all_to_all.40.refs_1_, bf16[2,16,16,64,128]{4,3,2,1,0:T(8,128)(2,1)} %refs_2_.3, bf16[128,1536]{1,0:T(8,128)(2,1)} %constant.29.clone.refs_3_.refs_4_, ...), custom_call_target="tpu_custom_call" | custom-call | tf_op jit(solution)/shard_map/mix/pallas_call | solution.py:392
  139.7 52.5 %all_to_all.41.wire = f32[16,4,64,128]{3,2,1,0:T(8,128)} all-to-all(f32[16,4,64,128]{3,2,1,0:T(8,128)} %get-tuple-element.22), channel_id=1, replica_groups=mesh['groups'=2,'space'=16] {'space'}, dimensions={0} | all-to-all | bytes 4194304 | tf_op jit(solution)/shard_map/all_to_all | solution.py:558
  192.2 5.0 all-to-all-start.2
  197.2 0.0 copy-done.7
  197.2 0.0 copy-start.8
  197.2 0.1 copy.23
  197.3 0.2 multiply_convert_fusion.1
  197.6 1.7 convert_element_type.36.point
  199.2 0.0 copy-done.8
  199.2 0.1 broadcast_in_dim.23
  199.3 0.1 broadcast_in_dim.24
  199.4 0.8 broadcast_in_dim.25.bias
  200.1 34.4 %synthesise.2 = (bf16[16,16,256,128]{3,2,1,0:T(8,128)(2,1)}, bf16[16,16,256,128]{3,2,1,0:T(8,128)(2,1)}, f32[16,4,64,128]{3,2,1,0:T(8,128)}, f32[256,256]{1,0:T(8,128)}, f32[256,128]{1,0:T(8,128)}) custom-call(f32[16,4,64,128]{3,2,1,0:T(8,128)} %all_to_all.41.wire, bf16[16,16,256,128]{3,2,1,0:T(8,128)(2,1)} %bitcast.15, bf16[16,16,256,128]{3,2,1,0:T(8,128)(2,1)} %bitcast.18, ...), custom_call_target="tpu_custom_call" | custom-call | tf_op jit(solution)/shard_map/synthesise/pallas_call | solution.py:501
  234.5 10.4 %all-to-all-done.2.wire = f32[16,4,64,128]{3,2,1,0:T(8,128)S(1)} async-done(((f32[16,4,64,128]{3,2,1,0:T(8,128)}), f32[16,4,64,128]{3,2,1,0:T(8,128)S(1)}, u32[]{:S(2)}, u32[]{:S(2)}) %all-to-all-start.2) | async-done | bytes 2097184 | tf_op jit(solution)/shard_map/all_to_all | solution.py:558
  244.9 1.3 copy-done.1
  246.2 4.7 all-to-all-start.4
  250.9 34.4 %synthesise.3 = (bf16[16,16,256,128]{3,2,1,0:T(8,128)(2,1)}, bf16[16,16,256,128]{3,2,1,0:T(8,128)(2,1)}, f32[16,4,64,128]{3,2,1,0:T(8,128)}, f32[256,256]{1,0:T(8,128)}, f32[256,128]{1,0:T(8,128)}) custom-call(f32[16,4,64,128]{3,2,1,0:T(8,128)} %copy-done.1, bf16[16,16,256,128]{3,2,1,0:T(8,128)(2,1)} %bitcast.16, ...), custom_call_target="tpu_custom_call", output_to_operand_aliasing={{0}: (9, {}), {1}: (10, {})} | custom-call | tf_op jit(solution)/shard_map/synthesise/pallas_call | solution.py:501
  285.3 13.3 %all-to-all-done.4.refs_0_ = f32[16,4,64,128]{3,2,1,0:T(8,128)} async-done(((f32[16,4,64,128]{3,2,1,0:T(8,128)}), f32[16,4,64,128]{3,2,1,0:T(8,128)}, u32[]{:S(2)}, u32[]{:S(2)}) %all-to-all-start.4) | async-done | bytes 2097184 | tf_op jit(solution)/shard_map/all_to_all | solution.py:558
  298.6 4.8 all-to-all-start.5
  303.4 0.0 copy-done.5
  303.4 0.0 copy-done.6
  303.5 0.1 add_reduce_fusion
  303.6 0.1 reduce_sum.36
  303.7 0.0 copy-done.3
  303.7 0.0 copy-done.4
  303.7 0.6 reshape.49
  304.4 0.4 multiply_convert_fusion
  304.7 0.1 reshape.50
  304.8 0.1 reduce_sum.37
  304.9 0.6 fusion.refs_6_
  305.5 45.7 %all-to-all-done.5.refs_1_ = f32[16,4,64,128]{3,2,1,0:T(8,128)} async-done(((f32[16,4,64,128]{3,2,1,0:T(8,128)}), f32[16,4,64,128]{3,2,1,0:T(8,128)}, u32[]{:S(2)}, u32[]{:S(2)}) %all-to-all-start.5) | async-done | bytes 2097184 | tf_op jit(solution)/shard_map/all_to_all | solution.py:558
  351.2 22.9 %dual.1 = (f32[16,4,64,128]{3,2,1,0:T(8,128)}, f32[16,4,72,128]{3,2,1,0:T(8,128)}, f32[2,16,16,64,128]{4,3,2,1,0:T(8,128)}) custom-call(f32[16,4,64,128]{3,2,1,0:T(8,128)} %all-to-all-done.4.refs_0_, f32[16,4,64,128]{3,2,1,0:T(8,128)} %all-to-all-done.5.refs_1_, bf16[2,16,16,64,128]{4,3,2,1,0:T(8,128)(2,1)} %refs_2_.3, ...), custom_call_target="tpu_custom_call" | custom-call | tf_op jit(solution)/shard_map/dual/pallas_call | solution.py:407
  374.1 52.4 %all_to_all.42.wire = f32[16,4,64,128]{3,2,1,0:T(8,128)} all-to-all(f32[16,4,64,128]{3,2,1,0:T(8,128)} %get-tuple-element.35), channel_id=1, replica_groups=mesh['groups'=2,'space'=16] {'space'}, dimensions={0} | all-to-all | bytes 4194304 | tf_op jit(solution)/shard_map/all_to_all | solution.py:558
  426.5 4.8 all-to-all-start.6
  431.3 1.7 convert_element_type.39.point
  433.0 15.8 %finish.2.refs_0_ = bf16[16,16,256,128]{3,2,1,0:T(8,128)(2,1)} custom-call(f32[16,4,64,128]{3,2,1,0:T(8,128)} %all_to_all.42.wire, bf16[16,16,256,128]{3,2,1,0:T(8,128)(2,1)} %get-tuple-element.34.grad, bf16[256,256]{1,0:T(8,128)(2,1)} %convert_element_type.39.point, bf16[512,128]{1,0:T(8,128)(2,1)} %constant.28.clone.y_up, bf16[256,512]{1,0:T(8,128)(2,1)} %constant.25.clone.z_up), custom_call_target="tpu_custom_call" | custom-call | tf_op jit(solution)/shard_map/finish/pallas_call | solution.py:544
  448.7 35.9 %all-to-all-done.6.wire = f32[16,4,72,128]{3,2,1,0:T(8,128)S(1)} async-done(((f32[16,4,72,128]{3,2,1,0:T(8,128)}), f32[16,4,72,128]{3,2,1,0:T(8,128)S(1)}, u32[]{:S(2)}, u32[]{:S(2)}) %all-to-all-start.6) | async-done | bytes 2359328 | tf_op jit(solution)/shard_map/all_to_all | solution.py:558
  484.6 0.1 slice.13
  484.7 0.7 slice_multiply_fusion
  485.4 0.5 slice_multiply_fusion.1
  486.0 0.0 copy-done
  486.0 15.8 %finish.3 = bf16[16,16,256,128]{3,2,1,0:T(8,128)(2,1)} custom-call(f32[16,4,72,128]{3,2,1,0:T(8,128)} %copy-done, bf16[16,16,256,128]{3,2,1,0:T(8,128)(2,1)} %get-tuple-element.34.grad, bf16[256,256]{1,0:T(8,128)(2,1)} %convert_element_type.39.point, bf16[512,128]{1,0:T(8,128)(2,1)} %constant.28.clone.y_up, ...), custom_call_target="tpu_custom_call", output_to_operand_aliasing={{}: (5, {})} | custom-call | tf_op jit(solution)/shard_map/finish/pallas_call | solution.py:544
  (12 shorter events, 0.1 us)
Async XLA Ops:
  13.0 53.8 %all-to-all-start = ((f32[16,4,64,128]{3,2,1,0:T(8,128)}), f32[16,4,64,128]{3,2,1,0:T(8,128)S(1)}, u32[]{:S(2)}, u32[]{:S(2)}) async-start(f32[16,4,64,128]{3,2,1,0:T(8,128)} %analyse.2), calls=%async_computation | async-start | bytes 4194304 | tf_op jit(solution)/shard_map/all_to_all | solution.py:558
  66.8 52.4 %copy-start.2 = (f32[16,4,64,128]{3,2,1,0:T(8,128)}, f32[16,4,64,128]{3,2,1,0:T(8,128)S(1)}, u32[]{:S(2)}) copy-start(f32[16,4,64,128]{3,2,1,0:T(8,128)S(1)} %all-to-all-done.refs_0_) | copy-start | bytes 6291460
  192.2 5.0 copy-start.7
  192.2 52.6 %all-to-all-start.2 = ((f32[16,4,64,128]{3,2,1,0:T(8,128)}), f32[16,4,64,128]{3,2,1,0:T(8,128)S(1)}, u32[]{:S(2)}, u32[]{:S(2)}) async-start(f32[16,4,64,128]{3,2,1,0:T(8,128)} %get-tuple-element.21), calls=%async_computation.2 | async-start | bytes 4194304 | tf_op jit(solution)/shard_map/all_to_all | solution.py:558
  197.2 2.0 copy-start.8
  244.9 1.3 copy-start.1
  246.2 52.4 %all-to-all-start.4 = ((f32[16,4,64,128]{3,2,1,0:T(8,128)}), f32[16,4,64,128]{3,2,1,0:T(8,128)}, u32[]{:S(2)}, u32[]{:S(2)}) async-start(f32[16,4,64,128]{3,2,1,0:T(8,128)} %get-tuple-element.26), calls=%async_computation.4 | async-start | bytes 4194304 | tf_op jit(solution)/shard_map/all_to_all | solution.py:558
  298.6 4.8 copy-start.5
  298.6 4.8 copy-start.6
  298.6 5.0 %copy-start.3 = (f32[256,256]{1,0:T(8,128)S(1)}, f32[256,256]{1,0:T(8,128)}, u32[]{:S(2)}) copy-start(f32[256,256]{1,0:T(8,128)} %get-tuple-element.29) | copy-start | bytes 786436
  298.6 5.0 %copy-start.4 = (f32[256,256]{1,0:T(8,128)S(1)}, f32[256,256]{1,0:T(8,128)}, u32[]{:S(2)}) copy-start(f32[256,256]{1,0:T(8,128)} %get-tuple-element.30) | copy-start | bytes 786436
  298.6 52.6 %all-to-all-start.5 = ((f32[16,4,64,128]{3,2,1,0:T(8,128)}), f32[16,4,64,128]{3,2,1,0:T(8,128)}, u32[]{:S(2)}, u32[]{:S(2)}) async-start(f32[16,4,64,128]{3,2,1,0:T(8,128)} %get-tuple-element.27), calls=%async_computation.5 | async-start | bytes 4194304 | tf_op jit(solution)/shard_map/all_to_all | solution.py:558
  426.5 58.1 %all-to-all-start.6 = ((f32[16,4,72,128]{3,2,1,0:T(8,128)}), f32[16,4,72,128]{3,2,1,0:T(8,128)S(1)}, u32[]{:S(2)}, u32[]{:S(2)}) async-start(f32[16,4,72,128]{3,2,1,0:T(8,128)} %get-tuple-element.33), calls=%async_computation.6 | async-start | bytes 4718592 | tf_op jit(solution)/shard_map/all_to_all | solution.py:558
  484.6 1.4 copy-start

commit v3 on v2

--- a/solution.py
+++ b/solution.py
@@ -249,7 +249,7 @@
 
 def analyse_call(field, z_table, y_table, spaces, chunk):
     channels, planes, cells_y, cells_z = field.shape
-    part = planes // CHUNKS
+    part = planes
     step = min(4, part)
     return pl.pallas_call(
         analyse_kernel,
@@ -312,10 +312,10 @@
 
 
 def mix_kernel(*refs):
-    wires = refs[:CHUNKS]
-    weight, x_down, x_up = refs[CHUNKS : CHUNKS + 3]
-    outs = refs[CHUNKS + 3 : 2 * CHUNKS + 3]
-    kept, spectrum, mixed = refs[2 * CHUNKS + 3 :]
+    wires = refs[:1]
+    weight, x_down, x_up = refs[1:4]
+    outs = refs[4 : CHUNKS + 4]
+    kept, spectrum, mixed = refs[CHUNKS + 4 :]
     step = pl.program_id(0)
     channels = spectrum.shape[0]
     half = spectrum.shape[1] // 2
@@ -377,12 +377,13 @@
 
 def mix_call(wires, weight, kept, sums, x_down, x_up):
     _, channels, _, modes_x, modes = weight.shape
+    wire_specs = [fixed(wire.shape) for wire in wires]
     shape = wires[0].shape
+    shape = shape[:2] + (shape[2] * len(wires) // CHUNKS, shape[3])
     wire_block = (shape[0], 1) + shape[2:]
-    wire_specs = [fixed(shape) for _ in wires]
     tables = [fixed(x_down.shape), fixed(x_up.shape)]
-    out_wires = [pl.BlockSpec(wire_block, lambda s: (0, s // GROUP, 0, 0)) for _ in wires]
-    out_shapes = [jax.ShapeDtypeStruct(shape, F32) for _ in wires]
+    out_wires = [pl.BlockSpec(wire_block, lambda s: (0, s // GROUP, 0, 0)) for _ in range(CHUNKS)]
+    out_shapes = [jax.ShapeDtypeStruct(shape, F32) for _ in range(CHUNKS)]
     scratch = [
         pltpu.VMEM((channels, 2 * modes_x, modes), F32),
         pltpu.VMEM((GROUP, 2 * modes_x, modes), F32),
@@ -570,8 +571,9 @@
     point_out = jnp.kron(point_weight.astype(F32), eye).astype(BF16)
     bias_rows = jnp.broadcast_to(jnp.repeat(bias, ROWS)[:, None], (channels * ROWS, cells_z))
     chunks = range(CHUNKS)
-    wires = [exchange(analyse_call(field_part, z_down, y_down, spaces, h)) for h in chunks]
-    *wires, kept = mix_call(wires, spectral_weight, None, None, x_down, x_up)
+    wires = [exchange(analyse_call(field_part, z_down, y_down, spaces, 0))]
+    x_whole = jnp.asarray(blocked_tables(cells_x, cells_y, cells_z, spaces, 1)[6])
+    *wires, kept = mix_call(wires, spectral_weight, None, None, x_whole, x_up)
     wires = [exchange(w) for w in wires]
     earlier, back, point_sums, bias_sums = [], [], 0.0, 0.0
     for h in chunks:

time: 504 us -> 507 us (level)
  blocking collectives: 157 us -> 204 us
  waiting for transfers between devices: 140 us -> 105 us
  starting transfers between devices: 25.5 us -> 19.3 us
    all_to_all x3, blocking collectives: 157 us -> 204 us  [exchange(): lax.all_to_all(values, 'space', split_axis=0, concat_axis=0, tiled=True)]
    all_to_all x5 -> x4, waiting for transfers between devices: 140 us -> 105 us  [exchange(): lax.all_to_all(values, 'space', split_axis=0, concat_axis=0, tiled=True)]
    all_to_all x5 -> x4, starting transfers between devices: 25.5 us -> 19.3 us  [exchange(): lax.all_to_all(values, 'space', split_axis=0, concat_axis=0, tiled=True)]
    pallas_call x2 -> x1, Pallas kernels: 24.7 us -> 22.7 us  [analyse_call(): pl.pallas_call(analyse_kernel, grid=(channels // GROUP, part // step), in...]
  transfers between devices with their start and end apart: 5 -> 4, of which waited for: 5 -> 4; matrix products, arithmetic and copies ran while one was open for 1% -> 1% of each run, Pallas kernels for 19% -> 17%
where the time goes in v3:
time: 507 us; the launch traced here: 505 us
  blocking collectives  204 us (40%)
  Pallas kernels  166 us (33%)
  waiting for transfers between devices  105 us (21%)
  starting transfers between devices  19.3 us (4%)
  local copies, waits for them, and re-layouts  6.56 us (1%)
    all_to_all x3, blocking collectives, exchange(): lax.all_to_all(values, 'space', split_axis=0, concat_axis=0, tiled=True)  204 us
    all_to_all x4, waiting for transfers between devices, exchange(): lax.all_to_all(values, 'space', split_axis=0, concat_axis=0, tiled=True)  105 us
    pallas_call x2, Pallas kernels, synthesise_call(): pl.pallas_call(synthesise_kernel, grid=(part,), in_specs=specs, out_specs...  68.8 us
    pallas_call x2, Pallas kernels, finish_call(): pl.pallas_call(finish_kernel, grid=(part,), in_specs=specs, out_specs=sla...  31.5 us
    pallas_call x1, Pallas kernels, mix_call(): pl.pallas_call(dual_kernel, grid=(channels,), in_specs=wire_specs + [pl.B...  22.9 us
    pallas_call x1, Pallas kernels, analyse_call(): pl.pallas_call(analyse_kernel, grid=(channels // GROUP, part // step), in...  22.7 us
    pallas_call x1, Pallas kernels, mix_call(): pl.pallas_call(mix_kernel, grid=(channels,), in_specs=wire_specs + [pl.Bl...  20.5 us
    all_to_all x4, starting transfers between devices, exchange(): lax.all_to_all(values, 'space', split_axis=0, concat_axis=0, tiled=True)  19.3 us
  transfers between devices with their start and end apart: 4, of which 4 were waited for; matrix products, arithmetic and copies ran while one was open for 1% of the time, Pallas kernels for 17%

profile of v3, /device:TPU:16, one launch (start us, length us, event | category | flops | bytes accessed | tf_op | source)
XLA Modules:
  0.0 504.8 jit_solution(12852633489958657919)
XLA Ops:
  0.6 22.7 %analyse.1 = f32[16,4,128,128]{3,2,1,0:T(8,128)} custom-call(bf16[16,16,256,128]{3,2,1,0:T(8,128)(2,1)} %bitcast.13, bf16[512,256]{1,0:T(8,128)(2,1)} %constant.10.clone.z_table, bf16[128,512]{1,0:T(8,128)(2,1)} %constant.29.clone.y_table.y_down), custom_call_target="tpu_custom_call" | custom-call | tf_op jit(solution)/shard_map/analyse/pallas_call | solution.py:254
  23.3 98.9 %all_to_all.35.refs_0_ = f32[16,4,128,128]{3,2,1,0:T(8,128)} all-to-all(f32[16,4,128,128]{3,2,1,0:T(8,128)} %analyse.1), channel_id=1, replica_groups=mesh['groups'=2,'space'=16] {'space'}, dimensions={0} | all-to-all | bytes 8388608 | tf_op jit(solution)/shard_map/all_to_all | solution.py:559
  122.2 20.5 %mix.1 = (f32[16,4,64,128]{3,2,1,0:T(8,128)}, f32[16,4,64,128]{3,2,1,0:T(8,128)}, bf16[16,128,128]{2,1,0:T(8,128)(2,1)}) custom-call(f32[16,4,128,128]{3,2,1,0:T(8,128)} %all_to_all.35.refs_0_, bf16[2,16,16,64,128]{4,3,2,1,0:T(8,128)(2,1)} %refs_2_.2, bf16[128,1536]{1,0:T(8,128)(2,1)} %constant.33.clone.refs_2_, bf16[512,384]{1,0:T(8,128)(2,1)} %constant.32.clone.refs_3_.refs_5_), custom_call_target="tpu_custom_call" | custom-call | tf_op jit(solution)/shard_map/mix/pallas_call | solution.py:393
  142.7 52.7 %all_to_all.36.wire = f32[16,4,64,128]{3,2,1,0:T(8,128)} all-to-all(f32[16,4,64,128]{3,2,1,0:T(8,128)} %get-tuple-element.22), channel_id=1, replica_groups=mesh['groups'=2,'space'=16] {'space'}, dimensions={0} | all-to-all | bytes 4194304 | tf_op jit(solution)/shard_map/all_to_all | solution.py:559
  195.3 0.0 copy-start.6
  195.3 5.0 all-to-all-start.1
  200.3 0.0 copy-done.6
  200.3 0.0 copy-start.7
  200.3 0.1 copy.24
  200.4 0.2 multiply_convert_fusion.1
  200.6 1.6 convert_element_type.36.point
  202.3 0.0 copy-done.7
  202.3 0.1 broadcast_in_dim.23
  202.4 0.1 broadcast_in_dim.24
  202.4 0.8 broadcast_in_dim.25.bias
  203.2 34.4 %synthesise.2 = (bf16[16,16,256,128]{3,2,1,0:T(8,128)(2,1)}, bf16[16,16,256,128]{3,2,1,0:T(8,128)(2,1)}, f32[16,4,64,128]{3,2,1,0:T(8,128)}, f32[256,256]{1,0:T(8,128)}, f32[256,128]{1,0:T(8,128)}) custom-call(f32[16,4,64,128]{3,2,1,0:T(8,128)} %all_to_all.36.wire, bf16[16,16,256,128]{3,2,1,0:T(8,128)(2,1)} %bitcast.14, bf16[16,16,256,128]{3,2,1,0:T(8,128)(2,1)} %bitcast.17, ...), custom_call_target="tpu_custom_call" | custom-call | tf_op jit(solution)/shard_map/synthesise/pallas_call | solution.py:502
  237.6 10.4 %all-to-all-done.1.wire = f32[16,4,64,128]{3,2,1,0:T(8,128)S(1)} async-done(((f32[16,4,64,128]{3,2,1,0:T(8,128)}), f32[16,4,64,128]{3,2,1,0:T(8,128)S(1)}, u32[]{:S(2)}, u32[]{:S(2)}) %all-to-all-start.1) | async-done | bytes 2097184 | tf_op jit(solution)/shard_map/all_to_all | solution.py:559
  247.9 0.0 copy-start.1
  247.9 1.3 copy-done.1
  249.3 4.7 all-to-all-start.3
  253.9 34.5 %synthesise.3 = (bf16[16,16,256,128]{3,2,1,0:T(8,128)(2,1)}, bf16[16,16,256,128]{3,2,1,0:T(8,128)(2,1)}, f32[16,4,64,128]{3,2,1,0:T(8,128)}, f32[256,256]{1,0:T(8,128)}, f32[256,128]{1,0:T(8,128)}) custom-call(f32[16,4,64,128]{3,2,1,0:T(8,128)} %copy-done.1, bf16[16,16,256,128]{3,2,1,0:T(8,128)(2,1)} %bitcast.15, ...), custom_call_target="tpu_custom_call", output_to_operand_aliasing={{0}: (9, {}), {1}: (10, {})} | custom-call | tf_op jit(solution)/shard_map/synthesise/pallas_call | solution.py:502
  288.4 13.3 %all-to-all-done.3.refs_0_ = f32[16,4,64,128]{3,2,1,0:T(8,128)} async-done(((f32[16,4,64,128]{3,2,1,0:T(8,128)}), f32[16,4,64,128]{3,2,1,0:T(8,128)}, u32[]{:S(2)}, u32[]{:S(2)}) %all-to-all-start.3) | async-done | bytes 2097184 | tf_op jit(solution)/shard_map/all_to_all | solution.py:559
  301.7 0.0 copy-start.4
  301.7 0.0 copy-start.5
  301.7 4.8 all-to-all-start.4
  306.5 0.0 copy-done.4
  306.5 0.0 copy-done.5
  306.5 0.1 add_reduce_fusion
  306.6 0.1 reduce_sum.36
  306.7 0.0 copy-done.2
  306.7 0.0 copy-done.3
  306.8 0.6 reshape.49
  307.4 0.4 multiply_convert_fusion
  307.8 0.1 reshape.50
  307.9 0.1 reduce_sum.37
  308.0 0.6 fusion.refs_6_
  308.6 45.7 %all-to-all-done.4.refs_1_ = f32[16,4,64,128]{3,2,1,0:T(8,128)} async-done(((f32[16,4,64,128]{3,2,1,0:T(8,128)}), f32[16,4,64,128]{3,2,1,0:T(8,128)}, u32[]{:S(2)}, u32[]{:S(2)}) %all-to-all-start.4) | async-done | bytes 2097184 | tf_op jit(solution)/shard_map/all_to_all | solution.py:559
  354.3 22.9 %dual.1 = (f32[16,4,64,128]{3,2,1,0:T(8,128)}, f32[16,4,72,128]{3,2,1,0:T(8,128)}, f32[2,16,16,64,128]{4,3,2,1,0:T(8,128)}) custom-call(f32[16,4,64,128]{3,2,1,0:T(8,128)} %all-to-all-done.3.refs_0_, f32[16,4,64,128]{3,2,1,0:T(8,128)} %all-to-all-done.4.refs_1_, bf16[2,16,16,64,128]{4,3,2,1,0:T(8,128)(2,1)} %refs_2_.2, ...), custom_call_target="tpu_custom_call" | custom-call | tf_op jit(solution)/shard_map/dual/pallas_call | solution.py:408
  377.2 52.4 %all_to_all.37.wire = f32[16,4,64,128]{3,2,1,0:T(8,128)} all-to-all(f32[16,4,64,128]{3,2,1,0:T(8,128)} %get-tuple-element.35), channel_id=1, replica_groups=mesh['groups'=2,'space'=16] {'space'}, dimensions={0} | all-to-all | bytes 4194304 | tf_op jit(solution)/shard_map/all_to_all | solution.py:559
  429.5 4.8 all-to-all-start.5
  434.4 1.6 convert_element_type.39.point
  436.0 15.8 %finish.2.refs_0_ = bf16[16,16,256,128]{3,2,1,0:T(8,128)(2,1)} custom-call(f32[16,4,64,128]{3,2,1,0:T(8,128)} %all_to_all.37.wire, bf16[16,16,256,128]{3,2,1,0:T(8,128)(2,1)} %get-tuple-element.34.grad, bf16[256,256]{1,0:T(8,128)(2,1)} %convert_element_type.39.point, bf16[512,128]{1,0:T(8,128)(2,1)} %constant.30.clone.y_up, bf16[256,512]{1,0:T(8,128)(2,1)} %constant.27.clone.z_up), custom_call_target="tpu_custom_call" | custom-call | tf_op jit(solution)/shard_map/finish/pallas_call | solution.py:545
  451.8 35.9 %all-to-all-done.5.wire = f32[16,4,72,128]{3,2,1,0:T(8,128)S(1)} async-done(((f32[16,4,72,128]{3,2,1,0:T(8,128)}), f32[16,4,72,128]{3,2,1,0:T(8,128)S(1)}, u32[]{:S(2)}, u32[]{:S(2)}) %all-to-all-start.5) | async-done | bytes 2359328 | tf_op jit(solution)/shard_map/all_to_all | solution.py:559
  487.7 0.1 slice.13
  487.8 0.7 slice_multiply_fusion
  488.5 0.5 slice_multiply_fusion.1
  489.0 0.1 copy-done
  489.1 15.8 %finish.3 = bf16[16,16,256,128]{3,2,1,0:T(8,128)(2,1)} custom-call(f32[16,4,72,128]{3,2,1,0:T(8,128)} %copy-done, bf16[16,16,256,128]{3,2,1,0:T(8,128)(2,1)} %get-tuple-element.34.grad, bf16[256,256]{1,0:T(8,128)(2,1)} %convert_element_type.39.point, bf16[512,128]{1,0:T(8,128)(2,1)} %constant.30.clone.y_up, ...), custom_call_target="tpu_custom_call", output_to_operand_aliasing={{}: (5, {})} | custom-call | tf_op jit(solution)/shard_map/finish/pallas_call | solution.py:545
  (7 shorter events, 0.1 us)
Async XLA Ops:
  195.3 5.0 copy-start.6
  195.3 52.6 %all-to-all-start.1 = ((f32[16,4,64,128]{3,2,1,0:T(8,128)}), f32[16,4,64,128]{3,2,1,0:T(8,128)S(1)}, u32[]{:S(2)}, u32[]{:S(2)}) async-start(f32[16,4,64,128]{3,2,1,0:T(8,128)} %get-tuple-element.21), calls=%async_computation.1 | async-start | bytes 4194304 | tf_op jit(solution)/shard_map/all_to_all | solution.py:559
  200.3 2.0 copy-start.7
  247.9 1.3 copy-start.1
  249.3 52.4 %all-to-all-start.3 = ((f32[16,4,64,128]{3,2,1,0:T(8,128)}), f32[16,4,64,128]{3,2,1,0:T(8,128)}, u32[]{:S(2)}, u32[]{:S(2)}) async-start(f32[16,4,64,128]{3,2,1,0:T(8,128)} %get-tuple-element.26), calls=%async_computation.3 | async-start | bytes 4194304 | tf_op jit(solution)/shard_map/all_to_all | solution.py:559
  301.7 4.8 copy-start.4
  301.7 4.8 copy-start.5
  301.7 5.0 copy-start.2
  301.7 5.0 copy-start.3
  301.7 52.6 %all-to-all-start.4 = ((f32[16,4,64,128]{3,2,1,0:T(8,128)}), f32[16,4,64,128]{3,2,1,0:T(8,128)}, u32[]{:S(2)}, u32[]{:S(2)}) async-start(f32[16,4,64,128]{3,2,1,0:T(8,128)} %get-tuple-element.27), calls=%async_computation.4 | async-start | bytes 4194304 | tf_op jit(solution)/shard_map/all_to_all | solution.py:559
  429.5 58.1 %all-to-all-start.5 = ((f32[16,4,72,128]{3,2,1,0:T(8,128)}), f32[16,4,72,128]{3,2,1,0:T(8,128)S(1)}, u32[]{:S(2)}, u32[]{:S(2)}) async-start(f32[16,4,72,128]{3,2,1,0:T(8,128)} %get-tuple-element.33), calls=%async_computation.5 | async-start | bytes 4718592 | tf_op jit(solution)/shard_map/all_to_all | solution.py:559
  487.6 1.4 copy-start
